TPU v7x, 256 devices: a whole 4x4x8 slice. The times are simulated.
256 devices in a mesh: band: 16 (over z, core), gvec: 16 (over y, x).
Axes of the slice: x: 4, y: 4, z: 8, core: 2. Of those that a mesh axis runs over, the one named last changes fastest.
Arguments:
- pair_density: bfloat16 [768, 16, 60000], P('band', None, 'gvec'), may hold values from -6 to 6
- eigvecs: bfloat16 [60000, 2000], P('gvec', 'band'), may hold values from -0.0234375 to 0.0234375
- subspace: bfloat16 [4, 2000, 2000], P(None, 'gvec'), may hold values from -0.125 to 0.125
- counts: int32 [16], P('band'), may hold values from 1 to 48, as said below
- freq_index: int32 [768, 16], P('band'), may hold values from 0 to 3
- band_weight: float32 [768], P('band'), may hold values from 0.3 to 3
Outputs:
- coef: float32 [768, 16, 2000], P('band', None, 'gvec')
- sigma: float32 [16], replicated
Inputs may be any that keep to these rules, and one draw needn't show every extreme that they name: `counts`: each group has at least one live slot; some group has all 48 slots live.
All inputs are finite; a program needn't handle non-finite values.
Results may differ from a plain program's by a relative error of at most 0.0026.
Values may be sent and summed in bfloat16 or wider, within the bound.
No kernel may reach another device: no remote copies, remote signals or barrier semaphores. Data moves between devices by JAX's collectives and lax.ppermute only.
A program may use at most 128 MiB of HBM per device.

v0:
```python
import math

import jax
import jax.numpy as jnp
from jax import lax
from jax.experimental import pallas as pl
from jax.experimental.pallas import tpu as pltpu
from jax.sharding import PartitionSpec as P

NEIG = 2000
LANES = 128
LIMIT = 32000.0
STEPS = 24
SIDE = 4
GROUPS = ((0, 2), (2, 5))
SPLIT = 4
MEGA = 1024 * 1024
ANYWHERE = pl.BlockSpec(memory_space=pl.ANY)
IN_VMEM = pl.BlockSpec(memory_space=pltpu.VMEM)
IN_HBM = pl.BlockSpec(memory_space=pltpu.HBM)
IN_SMEM = pl.BlockSpec(memory_space=pltpu.SMEM)


def pin(value):
    return pltpu.with_memory_space_constraint(value, pltpu.HBM)


def spread_kernel(first_ref, w_ref, *outs):
    share = w_ref.shape[1]
    for side, ref in enumerate(outs):
        count, _, width = ref.shape
        ref[...] = jnp.zeros_like(ref)

        def one(n, carry, side=side, ref=ref):
            rows = w_ref[first_ref[side] + n]
            for k in range(width // LANES):
                ref[n, 0:share, k * LANES : k * LANES + share] = rows[:, k * share : (k + 1) * share]
            return carry

        lax.fori_loop(0, count, one, 0)


def spread(first, subspace):
    nodes, share, neig = subspace.shape
    half = jax.ShapeDtypeStruct((nodes // 2, LANES, neig // share * LANES), subspace.dtype)
    return pl.pallas_call(
        spread_kernel,
        in_specs=[IN_SMEM, IN_VMEM],
        out_specs=[IN_VMEM, IN_VMEM],
        out_shape=[half, half],
        compiler_params=pltpu.CompilerParams(vmem_limit_bytes=16 * MEGA),
        name="spread",
    )(first, subspace)


def project_kernel(shape, pd_ref, *refs):
    out_ref = refs[-1]
    at, columns = 0, []
    for count in shape:
        parts = [ref[...] for ref in refs[at : at + count]]
        columns.append(parts[0] if count == 1 else jnp.concatenate(parts, axis=0))
        at += count
    total = jnp.dot(pd_ref[...], jnp.concatenate(columns, axis=1), preferred_element_type=jnp.float32)
    most = jnp.max(jnp.abs(total), axis=1, keepdims=True)
    scale = jnp.ones_like(most)
    power = jnp.zeros(most.shape, jnp.int32)
    for j in range(1, STEPS + 1):
        fits = most * float(2**j) <= LIMIT
        scale = jnp.where(fits, float(2**j), scale)
        power = jnp.where(fits, j, power)
    code = jnp.round(total * scale).astype(jnp.int32)
    lane = lax.broadcasted_iota(jnp.int32, code.shape, 1)
    code = jnp.where(lane == LANES - 1, power, code).astype(jnp.int16)
    out_ref[...] = code.reshape(out_ref.shape)


def project(flat, blocks, devices, ahead=()):
    nrows, depth = flat.shape
    share = nrows // devices
    shape = [len(block) for block in blocks]
    parts = [part for block in blocks for part in block]
    width = len(blocks) * LANES
    return pl.pallas_call(
        lambda pd_ref, *refs: project_kernel(shape, pd_ref, *refs[: len(parts)], refs[-1]),
        grid=(SPLIT,),
        in_specs=[pl.BlockSpec((nrows // SPLIT, depth), lambda i: (i, 0))]
        + [pl.BlockSpec(part.shape, lambda i: (0, 0)) for part in parts]
        + [ANYWHERE] * len(ahead),
        out_specs=pl.BlockSpec((devices // SPLIT, share, width), lambda i: (i, 0, 0)),
        out_shape=pltpu.HBM((devices, share, width), jnp.int16),
        compiler_params=pltpu.CompilerParams(vmem_limit_bytes=32 * MEGA),
        cost_estimate=pl.CostEstimate(flops=10**6, bytes_accessed=10**4, transcendentals=0),
        name="project",
    )(pin(flat), *parts, *ahead)


def collect_kernel(count, live_ref, *refs):
    codes, coef_ref, rounded_ref = refs[:count], refs[count], refs[count + 1]
    at = 0
    for code_ref in codes:
        devices, rows, width = code_ref.shape
        total = jnp.zeros((rows, width), jnp.float32)
        for d in range(devices):
            power = code_ref[d, :, 0:LANES].astype(jnp.int32)[:, LANES - 1 : LANES]
            unit = 1.0 / (jnp.ones_like(power) << power).astype(jnp.float32)
            total += code_ref[d].astype(jnp.int32).astype(jnp.float32) * unit
        lane = lax.broadcasted_iota(jnp.int32, total.shape, 1)
        total = jnp.where(lane == LANES - 1, 0.0, total) * live_ref[...]
        for n in range(width // LANES):
            part = total[:, n * LANES : (n + 1) * LANES]
            coef_ref[at] = part
            rounded_ref[at] = part.astype(jnp.bfloat16)
            at += 1


def collect(codes, live_rows, ahead=()):
    rows = codes[0].shape[1]
    total = sum(code.shape[2] // LANES for code in codes)
    return pl.pallas_call(
        lambda *refs: collect_kernel(len(codes), *refs[: 1 + len(codes)], *refs[-2:]),
        in_specs=[IN_VMEM] * (1 + len(codes)) + [ANYWHERE] * len(ahead),
        out_specs=(IN_VMEM, IN_VMEM),
        out_shape=(
            jax.ShapeDtypeStruct((total, rows, LANES), jnp.float32),
            jax.ShapeDtypeStruct((total, rows, LANES), jnp.bfloat16),
        ),
        compiler_params=pltpu.CompilerParams(vmem_limit_bytes=12 * MEGA),
        name="collect",
    )(live_rows, *codes, *ahead)


def quad_kernel(groups, tables, ids_ref, own_ref, node_ref, pick_ref, *refs):
    coefs, refs = refs[:groups], refs[groups:]
    pieces, refs = refs[: groups * SIDE], refs[groups * SIDE :]
    weights, (out_ref, flat, store, sems) = refs[:tables], refs[tables:]
    rows = coefs[0].shape[1]
    blocks = out_ref.shape[0]
    for i, ref in enumerate(weights):
        count = ref.shape[0]
        pltpu.make_async_copy(ref, store.at[i * count : (i + 1) * count], sems.at[i]).start()
    at = 0
    for g in range(groups):
        for n in range(coefs[g].shape[0]):
            k = ids_ref[at]
            out_ref[k, 0:rows, :] = coefs[g][n]
            lane = pl.ds(pl.multiple_of(k * LANES, LANES), LANES)
            for d in range(SIDE):
                flat[d * rows : (d + 1) * rows, lane] = pieces[g * SIDE + d][n]
            at += 1
    right = flat[...]
    count = weights[0].shape[0]

    def add(i, total):
        pltpu.make_async_copy(store.at[0:count], store.at[pl.ds(i * count, count)], sems.at[i]).wait()
        lane = pl.ds(pl.multiple_of(own_ref[i] * LANES, LANES), LANES)
        left = flat[:, lane].astype(jnp.float32).T
        applied = lax.dot_general(
            store[pl.ds(i * count, count)].reshape(count * LANES, store.shape[2]),
            right,
            (((1,), (1,)), ((), ())),
            preferred_element_type=jnp.float32,
        )
        for n in range(count):
            value = jnp.sum(left * applied[n * LANES : (n + 1) * LANES], axis=0, keepdims=True)
            total += value * pick_ref[pl.ds(node_ref[i] + n, 1), :]
        return total

    total = lax.fori_loop(0, tables, add, jnp.zeros((1, SIDE * rows), jnp.float32))
    first = jnp.zeros((8, LANES), jnp.float32)
    line = lax.broadcasted_iota(jnp.int32, (8, LANES), 0)
    rest = jnp.concatenate([total[:, LANES:], jnp.zeros((1, 2 * LANES - SIDE * rows), jnp.float32)], axis=1)
    first = jnp.where(line == 0, total[:, 0:LANES], jnp.where(line == 1, rest, 0.0))
    for k in range(blocks):
        out_ref[k, rows : rows + 8, :] = first


def quadratic(ids, own, nodes_at, pick, coefs, pieces, weights):
    rows = coefs[0].shape[1]
    blocks = sum(c.shape[0] for c in coefs)
    return pl.pallas_call(
        lambda *refs: quad_kernel(len(coefs), len(weights), *refs),
        in_specs=[IN_SMEM] * 3 + [IN_VMEM] * (1 + len(coefs) + len(pieces)) + [IN_HBM] * len(weights),
        out_specs=IN_VMEM,
        out_shape=jax.ShapeDtypeStruct((blocks, rows + 8, LANES), jnp.float32),
        scratch_shapes=[
            pltpu.VMEM((SIDE * rows, blocks * LANES), jnp.bfloat16),
            pltpu.VMEM((sum(w.shape[0] for w in weights), LANES, blocks * LANES), jnp.bfloat16),
            pltpu.SemaphoreType.DMA((len(weights),)),
        ],
        compiler_params=pltpu.CompilerParams(vmem_limit_bytes=20 * MEGA),
        name="quad",
    )(ids, own, nodes_at, pick, *coefs, *pieces, *map(pin, weights))


def local(pair_density, eigvecs, subspace, counts, freq_index, band_weight):
    slots, states, depth = pair_density.shape
    nodes, share, neig = subspace.shape
    devices = lax.axis_size("gvec")
    bands = lax.axis_size("band")
    chips = bands // 2
    nrows = slots * states
    rows = nrows // devices
    band, gvec = lax.axis_index("band"), lax.axis_index("gvec")
    zed, core = band >> 1, band & 1
    why, ex = gvec >> 2, gvec & 3

    def shift(value, by):
        return lax.ppermute(value, "band", [(b, (b + 2 * by) % bands) for b in range(bands)])

    def sibling(value):
        return lax.ppermute(value, "band", [(b, b ^ 1) for b in range(bands)])

    def along_y(value, by):
        return lax.ppermute(value, "gvec", [(g, (g + SIDE * by) % devices) for g in range(devices)])

    def along_x(value):
        pairs = []
        for b in range(bands):
            for g in range(devices):
                to = g // SIDE * SIDE + (g + (1 if b % 2 == 0 else -1)) % SIDE
                pairs.append((b * devices + g, b * devices + to))
        return lax.ppermute(value, ("band", "gvec"), pairs)

    def along_z(value):
        return lax.ppermute(value, "band", [(b, (b + (2 if b % 2 == 0 else -2)) % bands) for b in range(bands)])

    flat = pair_density.reshape(nrows, depth)
    there, pair = 1 - core, nodes // 2
    turn = 2 * core - 1
    here, beside = core * pair, there * pair
    first_node = jnp.stack([here, beside]).astype(jnp.int32)
    nodes_at = jnp.stack([here, beside, here, beside, beside, here, here, beside]).astype(jnp.int32)
    x_at = [ex + d for d in (0, 0, turn, turn, -turn, -turn, 2, 2)]
    own = jnp.stack([why * SIDE + (x & (SIDE - 1)) for x in x_at]).astype(jnp.int32)

    steps = chips // 2
    places = [[zed]]
    for step in range(1, steps):
        places.append([(zed - step) & (chips - 1), (zed + step) & (chips - 1)])
    places.append([(zed + steps) & (chips - 1)])
    ids = []
    for begin, end in GROUPS:
        ids += [2 * z + c for step in range(begin, end) for z in places[step] for c in (core, there)]
    ids = jnp.stack(ids).astype(jnp.int32)


    def window(run, *operands):
        like = jax.eval_shape(run, *operands)
        return lax.cond(
            counts[0] > 0, run, lambda *_: jax.tree.map(lambda v: jnp.zeros(v.shape, v.dtype), like), *operands
        )

    def spread_rows(rounded):
        return [rounded] + [along_y(rounded, d) for d in range(1, SIDE)]

    def pair_up(blocks):
        return [part for block in blocks for part in (block, tuple(sibling(half) for half in block))]

    def send(code):
        return lax.all_to_all(code, "gvec", 0, 0)

    def first(flat, eigvecs, subspace, band_weight, freq_index):
        mine = jnp.pad(eigvecs, ((0, 0), (0, LANES - share)))
        up, down = shift(mine, 1), shift(mine, -1)
        table = spread(first_node, subspace)
        near = along_x(table[0])
        code = project(flat, pair_up([(mine,)]), devices)
        live = (jnp.arange(slots, dtype=jnp.int32) < counts[0]).astype(jnp.float32)
        live_rows = jnp.repeat(live, states).reshape(devices, rows, 1)
        weight_rows = jnp.repeat(band_weight * live, states).reshape(devices, rows)
        freq_rows = freq_index.reshape(devices, rows)
        order = [(((why - d) & (SIDE - 1)) * SIDE + ex) for d in range(SIDE)]
        freq_here = jnp.concatenate([lax.dynamic_index_in_dim(freq_rows, p, 0, False) for p in order])
        weight_here = jnp.concatenate([lax.dynamic_index_in_dim(weight_rows, p, 0, False) for p in order])
        pick = jnp.where(
            freq_here[None, :] == jnp.arange(nodes, dtype=jnp.int32)[:, None], weight_here[None, :], jnp.float32(0.0)
        )
        live_here = lax.dynamic_index_in_dim(live_rows, gvec, 0, False)

        return up, down, code, table, near, pick, live_here

    def middle(flat, up, down, code, rows_out):
        code_now = project(flat, pair_up([(up,), (down,)]), devices)
        return shift(up, 1), shift(down, -1), code_now, send(code), along_x(rows_out)

    def fourth(flat, up, down, code, landing, live_here):
        far = along_z(jnp.where(core == 0, up, down))
        coef, rounded = collect(landing, live_here)
        return far, project(flat, pair_up([(up,), (down,)]), devices), send(code), coef, rounded

    def fifth(flat, far, code, rounded, near, farther):
        swapped = [sibling(near), sibling(farther)]
        return send(project(flat, pair_up([(far,)]), devices)), send(code), spread_rows(rounded), swapped

    def sixth(landing, live_here, across):
        coef, rounded = collect(landing, live_here)
        return coef, spread_rows(rounded), sibling(across)

    up, down, code, table, near, pick, live_here = window(first, flat, eigvecs, subspace, band_weight, freq_index)
    up, down, code, landed_0, across = window(middle, flat, up, down, code, near)
    up, down, code, landed_1, farther = window(middle, flat, up, down, code, table[1])
    far, code, landed_2, coef_a, rounded = window(fourth, flat, up, down, code, [landed_0, landed_1], live_here)
    landed_4, landed_3, pieces_a, swapped = window(fifth, flat, far, code, rounded, near, farther)
    coef_b, pieces_b, across_swapped = window(sixth, [landed_2, landed_3, landed_4], live_here, across)
    weights = [*table, near, farther, *swapped, across, across_swapped]
    coefs, pieces = [coef_a, coef_b], pieces_a + pieces_b
    message = quadratic(ids, own, nodes_at, pick, coefs, pieces, weights)
    landed = lax.all_to_all(message, "gvec", 0, 0)
    coef_out = landed[:, 0:rows, 0:share].reshape(slots, states, share)
    terms = jnp.sum(landed[:, rows : rows + 2, :], axis=0)
    terms = jnp.sum(terms.reshape(2 * LANES // states, states), axis=0)
    spread_terms = lax.all_to_all(jnp.broadcast_to(terms, (bands, states)), "band", 0, 0)
    total = jnp.sum(spread_terms, axis=0)
    scale_factor = math.sqrt(NEIG * bands * slots)
    sigma = -total / jnp.float32(scale_factor)
    return (coef_out, sigma)


def solution(mesh):
    in_specs = (
        P("band", None, "gvec"),
        P("gvec", "band"),
        P(None, "gvec", None),
        P("band"),
        P("band", None),
        P("band"),
    )
    out_specs = (P("band", None, "gvec"), P())
    return jax.shard_map(local, mesh=mesh, in_specs=in_specs, out_specs=out_specs, check_vma=False)
```

profile of v0, /device:TPU:1, one launch (start us, length us, event | category | flops | bytes accessed | tf_op | source)
XLA Modules:
  0.0 198.4 jit_solution(1918420907286620473)
XLA Ops:
  1.5 32.4 %conditional.6 = (bf16[3750,128]{1,0:T(8,128)(2,1)}, bf16[3750,128]{1,0:T(8,128)(2,1)}, s16[16,48,256]{2,1,0:T(8,128)(2,1)}, bf16[2,128,2048]{2,1,0:T(8,128)(2,1...) conditional(s32[]{:T(128)} %bitcast.32, () %tuple.56, ...), branch_computations={%region_0.0_spmd, %region_1.2_spmd} | conditional | flops 1003006 | bytes 21678728 | solution.py:249
  2.9 3.3 %collective-permute-start.22 = (bf16[3750,128]{1,0:T(8,128)(2,1)S(1)}, bf16[3750,128]{1,0:T(8,128)(2,1)S(1)}, u32[]{:S(2)}, u32[]{:S(2)}) collective-permute-start(bf16[3750,128]{1,0:T(8,128)(2,1)S(1)} %pad.3.refs_0_), channel_id=1, source_target_pairs={{0,16},{16,0},{32,48},{48,32},{64,80},{80,64},{96,112},{112,96},{1... | collective-permute-start | bytes 2880008 | tf_op jit(solution)/shard_map/cond/branch_1_fun/ppermute | solution.py:211
  6.2 3.9 %collective-permute-start.21 = (bf16[3750,128]{1,0:T(8,128)(2,1)S(1)}, bf16[3750,128]{1,0:T(8,128)(2,1)}, u32[]{:S(2)}, u32[]{:S(2)}) collective-permute-start(bf16[3750,128]{1,0:T(8,128)(2,1)S(1)} %pad.3.refs_0_), channel_id=1, source_target_pairs={{0,224},{16,240},{32,0},{48,16},{64,32},{80,48},{96,64},{112,80},{... | collective-permute-start | bytes 2880008 | tf_op jit(solution)/shard_map/cond/branch_1_fun/ppermute | solution.py:208
  12.8 3.0 %spread.1 = (bf16[2,128,2048]{2,1,0:T(8,128)(2,1)}, bf16[2,128,2048]{2,1,0:T(8,128)(2,1)S(1)}) custom-call(s32[2]{0:T(128)S(1)} %get-tuple-element.80.first_ref, bf16[4,125,2000]{2,1,0:T(8,128)(2,1)S(1)} %copy.24.w_ref), custom_call_target="tpu_custom_call" | custom-call | tf_op jit(solution)/shard_map/cond/branch_1_fun/spread/pallas_call | solution.py:46
  20.4 6.4 %project.5 = s16[16,48,256]{2,1,0:T(8,128)(2,1)} custom-call(bf16[768,3750]{1,0:T(8,128)(2,1)} %get-tuple-element.79.pd_ref, bf16[3750,128]{1,0:T(8,128)(2,1)S(1)} %pad.3.refs_0_, bf16[3750,128]{1,0:T(8,128)(2,1)S(1)} %collective-permute-done.22.refs_1_), custom_call_target="tpu_custom_call" | custom-call | flops 1000000 | bytes 10000 | tf_op jit(solution)/shard_map/cond/branch_1_fun/project/pallas_call | solution.py:83
  26.8 4.0 %collective-permute-done.21 = bf16[3750,128]{1,0:T(8,128)(2,1)} collective-permute-done((bf16[3750,128]{1,0:T(8,128)(2,1)S(1)}, bf16[3750,128]{1,0:T(8,128)(2,1)}, u32[]{:S(2)}, u32[]{:S(2)}) %collective-permute-start.21) | collective-permute-done | bytes 960032 | tf_op jit(solution)/shard_map/cond/branch_1_fun/ppermute | solution.py:208
  30.7 3.2 %collective-permute-done.20 = bf16[3750,128]{1,0:T(8,128)(2,1)} collective-permute-done((bf16[3750,128]{1,0:T(8,128)(2,1)S(1)}, bf16[3750,128]{1,0:T(8,128)(2,1)}, u32[]{:S(2)}, u32[]{:S(2)}) %collective-permute-start.20) | collective-permute-done | bytes 960032 | tf_op jit(solution)/shard_map/cond/branch_1_fun/ppermute | solution.py:208
  33.9 27.2 %conditional.7 = (bf16[3750,128]{1,0:T(8,128)(2,1)}, bf16[3750,128]{1,0:T(8,128)(2,1)}, s16[16,48,512]{2,1,0:T(8,128)(2,1)}, s16[16,48,256]{2,1,0:T(8,128)(2,1)}, bf16[2,128,2048]{2,1,0:T(8,128)(2,1)}) conditional(s32[]{:T(128)} %bitcast.32, () %tuple.60, (bf16[3750,128]{1,0:T(8,128)(2,1)}, bf16[3750,128]{1,0:T(8,128)(2,1)}, ...), branch_computations={%region_2.3_spmd, %region_3.4_spmd} | conditional | flops 1000000 | bytes 20744224 | solution.py:249
  39.6 6.2 %all-to-all-start = ((s16[16,48,256]{2,1,0:T(8,128)(2,1)}), s16[16,48,256]{2,1,0:T(8,128)(2,1)}, u32[]{:S(2)}, u32[]{:S(2)}) async-start(s16[16,48,256]{2,1,0:T(8,128)(2,1)} %get-tuple-element.93), calls=%async_computation | async-start | bytes 786432 | tf_op jit(solution)/shard_map/cond/branch_1_fun/all_to_all | solution.py:260
  45.8 8.1 %project.6 = s16[16,48,512]{2,1,0:T(8,128)(2,1)} custom-call(bf16[768,3750]{1,0:T(8,128)(2,1)} %get-tuple-element.92.pd_ref, bf16[3750,128]{1,0:T(8,128)(2,1)} %get-tuple-element.90.refs_0_, bf16[3750,128]{1,0:T(8,128)(2,1)S(1)} %collective-permute-done.2.refs_1_, bf16[3750,128]{1,0:T(8,128)(2,1)} %get-tuple-element.91.refs_2_, ...), custom_call_target="tpu_custom_call" | custom-call | flops 1000000 | bytes 10000 | tf_op jit(solution)/shard_map/cond/branch_1_fun/project/pallas_call | solution.py:83
  56.3 4.9 %collective-permute-done = bf16[3750,128]{1,0:T(8,128)(2,1)} collective-permute-done((bf16[3750,128]{1,0:T(8,128)(2,1)}, bf16[3750,128]{1,0:T(8,128)(2,1)}, u32[]{:S(2)}, u32[]{:S(2)}) %collective-permute-start) | collective-permute-done | bytes 960032 | tf_op jit(solution)/shard_map/cond/branch_1_fun/ppermute | solution.py:208
  61.1 26.3 %conditional.8 = (bf16[3750,128]{1,0:T(8,128)(2,1)}, bf16[3750,128]{1,0:T(8,128)(2,1)}, s16[16,48,512]{2,1,0:T(8,128)(2,1)}, s16[16,48,512]{2,1,0:T(8,128)(2,1)}, bf16[2,128,2048]{2,1,0:T(8,128)(2,1)}) conditional(s32[]{:T(128)} %bitcast.32, () %tuple.59, (bf16[3750,128]{1,0:T(8,128)(2,1)}, bf16[3750,128]{1,0:T(8,128)(2,1)}, ...), branch_computations={%region_4.5_spmd, %region_5.6_spmd} | conditional | flops 1000000 | bytes 21923872 | solution.py:249
  66.3 5.8 %all-to-all-start.1 = ((s16[16,48,512]{2,1,0:T(8,128)(2,1)}), s16[16,48,512]{2,1,0:T(8,128)(2,1)}, u32[]{:S(2)}, u32[]{:S(2)}) async-start(s16[16,48,512]{2,1,0:T(8,128)(2,1)} %get-tuple-element.98), calls=%async_computation.1 | async-start | bytes 1572864 | tf_op jit(solution)/shard_map/cond/branch_1_fun/all_to_all | solution.py:260
  72.1 8.1 %project.7 = s16[16,48,512]{2,1,0:T(8,128)(2,1)} custom-call(bf16[768,3750]{1,0:T(8,128)(2,1)} %get-tuple-element.97.pd_ref, bf16[3750,128]{1,0:T(8,128)(2,1)} %get-tuple-element.95.refs_0_, bf16[3750,128]{1,0:T(8,128)(2,1)S(1)} %collective-permute-done.7.refs_1_, bf16[3750,128]{1,0:T(8,128)(2,1)} %get-tuple-element.96.refs_2_, ...), custom_call_target="tpu_custom_call" | custom-call | flops 1000000 | bytes 10000 | tf_op jit(solution)/shard_map/cond/branch_1_fun/project/pallas_call | solution.py:83
  80.2 6.8 %all-to-all-done.1 = s16[16,48,512]{2,1,0:T(8,128)(2,1)} async-done(((s16[16,48,512]{2,1,0:T(8,128)(2,1)}), s16[16,48,512]{2,1,0:T(8,128)(2,1)}, u32[]{:S(2)}, u32[]{:S(2)}) %all-to-all-start.1) | async-done | bytes 786464 | tf_op jit(solution)/shard_map/cond/branch_1_fun/all_to_all | solution.py:260
  87.5 24.9 %conditional.9 = (bf16[3750,128]{1,0:T(8,128)(2,1)}, s16[16,48,512]{2,1,0:T(8,128)(2,1)}, s16[16,48,512]{2,1,0:T(8,128)(2,1)}, f32[6,48,128]{2,1,0:T(8,128)S(1)}, bf16[6,48,128]{2,1,0:T(8,128)(2,1)S(1)}) conditional(s32[]{:T(128)} %bitcast.32, () %tuple.58, (s32[]{:T(128)}, bf16[3750,128]{1,0:T(8,128)(2,1)}, bf16[3750,128]{1,0:T(8,128)(2,1)}, ...), branch_computations={%region_6.7_spmd, %region_7.8_spmd} | conditional | flops 1480001 | bytes 16769882 | solution.py:249
  93.4 5.5 %all-to-all-start.4 = ((s16[16,48,512]{2,1,0:T(8,128)(2,1)}), s16[16,48,512]{2,1,0:T(8,128)(2,1)}, u32[]{:S(2)}, u32[]{:S(2)}) async-start(s16[16,48,512]{2,1,0:T(8,128)(2,1)} %get-tuple-element.104), calls=%async_computation.4 | async-start | bytes 1572864 | tf_op jit(solution)/shard_map/cond/branch_1_fun/all_to_all | solution.py:260
  100.7 8.1 %project.8 = s16[16,48,512]{2,1,0:T(8,128)(2,1)} custom-call(bf16[768,3750]{1,0:T(8,128)(2,1)} %get-tuple-element.103.pd_ref, bf16[3750,128]{1,0:T(8,128)(2,1)} %get-tuple-element.101.refs_0_, bf16[3750,128]{1,0:T(8,128)(2,1)S(1)} %collective-permute-done.25.refs_1_, bf16[3750,128]{1,0:T(8,128)(2,1)} %get-tuple-element.102.refs_2_, ...), custom_call_target="tpu_custom_call" | custom-call | flops 1000000 | bytes 10000 | tf_op jit(solution)/shard_map/cond/branch_1_fun/project/pallas_call | solution.py:83
  108.8 3.5 %all-to-all-done.4 = s16[16,48,512]{2,1,0:T(8,128)(2,1)} async-done(((s16[16,48,512]{2,1,0:T(8,128)(2,1)}), s16[16,48,512]{2,1,0:T(8,128)(2,1)}, u32[]{:S(2)}, u32[]{:S(2)}) %all-to-all-start.4) | async-done | bytes 786464 | tf_op jit(solution)/shard_map/cond/branch_1_fun/all_to_all | solution.py:260
  112.4 35.0 %conditional.10 = (s16[16,48,256]{2,1,0:T(8,128)(2,1)}, s16[16,48,512]{2,1,0:T(8,128)(2,1)}, bf16[6,48,128]{2,1,0:T(8,128)(2,1)S(1)}, bf16[6,48,128]{2,1,0:T(8,1...) conditional(s32[]{:T(128)} %bitcast.32, () %tuple.65, ...), branch_computations={%region_8.9_spmd, %region_9.10_spmd} | conditional | flops 1000000 | bytes 16810112 | solution.py:249
  112.4 4.3 %all-to-all-start.3 = ((s16[16,48,512]{2,1,0:T(8,128)(2,1)}), s16[16,48,512]{2,1,0:T(8,128)(2,1)}, u32[]{:S(2)}, u32[]{:S(2)}) async-start(s16[16,48,512]{2,1,0:T(8,128)(2,1)} %get-tuple-element.112), calls=%async_computation.3 | async-start | bytes 1572864 | tf_op jit(solution)/shard_map/cond/branch_1_fun/all_to_all | solution.py:260
  117.4 6.7 %project.9 = s16[16,48,256]{2,1,0:T(8,128)(2,1)} custom-call(bf16[768,3750]{1,0:T(8,128)(2,1)} %get-tuple-element.110.pd_ref, bf16[3750,128]{1,0:T(8,128)(2,1)} %get-tuple-element.111.refs_0_, bf16[3750,128]{1,0:T(8,128)(2,1)S(1)} %collective-permute-done.10.refs_1_), custom_call_target="tpu_custom_call" | custom-call | flops 1000000 | bytes 10000 | tf_op jit(solution)/shard_map/cond/branch_1_fun/project/pallas_call | solution.py:83
  124.0 6.3 %all-to-all-done.3 = s16[16,48,512]{2,1,0:T(8,128)(2,1)} async-done(((s16[16,48,512]{2,1,0:T(8,128)(2,1)}), s16[16,48,512]{2,1,0:T(8,128)(2,1)}, u32[]{:S(2)}, u32[]{:S(2)}) %all-to-all-start.3) | async-done | bytes 786464 | tf_op jit(solution)/shard_map/cond/branch_1_fun/all_to_all | solution.py:260
  130.3 4.2 %all-to-all-start.2 = ((s16[16,48,256]{2,1,0:T(8,128)(2,1)}), s16[16,48,256]{2,1,0:T(8,128)(2,1)}, u32[]{:S(2)}, u32[]{:S(2)}) async-start(s16[16,48,256]{2,1,0:T(8,128)(2,1)} %project.9), calls=%async_computation.2 | async-start | bytes 786432 | tf_op jit(solution)/shard_map/cond/branch_1_fun/all_to_all | solution.py:260
  138.2 4.2 %collective-permute-done.13 = bf16[6,48,128]{2,1,0:T(8,128)(2,1)} collective-permute-done((bf16[6,48,128]{2,1,0:T(8,128)(2,1)S(1)}, bf16[6,48,128]{2,1,0:T(8,128)(2,1)}, u32[]{:S(2)}, u32[]{:S(2)}) %collective-permute-start.13) | collective-permute-done | bytes 73760 | tf_op jit(solution)/shard_map/cond/branch_1_fun/ppermute | solution.py:214
  147.4 13.7 %conditional.11 = (f32[10,48,128]{2,1,0:T(8,128)S(1)}, bf16[10,48,128]{2,1,0:T(8,128)(2,1)}, bf16[10,48,128]{2,1,0:T(8,128)(2,1)}, bf16[10,48,128]{2,1,0:T(8,128...) conditional(s32[]{:T(128)} %bitcast.32, () %tuple.64, (f32[48,1]{0,1:T(1,128)S(1)}, ...), branch_computations={%region_10.11_spmd, %region_11.12_spmd} | conditional | bytes 5669456 | solution.py:249
  152.4 3.8 %collective-permute-done.18 = bf16[10,48,128]{2,1,0:T(8,128)(2,1)} collective-permute-done((bf16[10,48,128]{2,1,0:T(8,128)(2,1)}, bf16[10,48,128]{2,1,0:T(8,128)(2,1)}, u32[]{:S(2)}, u32[]{:S(2)}) %collective-permute-start.18) | collective-permute-done | bytes 122912 | tf_op jit(solution)/shard_map/cond/branch_1_fun/ppermute | solution.py:214
  157.8 3.3 %collective-permute-done.16 = bf16[10,48,128]{2,1,0:T(8,128)(2,1)} collective-permute-done((bf16[10,48,128]{2,1,0:T(8,128)(2,1)}, bf16[10,48,128]{2,1,0:T(8,128)(2,1)}, u32[]{:S(2)}, u32[]{:S(2)}) %collective-permute-start.16) | collective-permute-done | bytes 122912 | tf_op jit(solution)/shard_map/cond/branch_1_fun/ppermute | solution.py:214
  161.3 6.3 %quad.1 = f32[16,56,128]{2,1,0:T(8,128)S(1)} custom-call(s32[16]{0:T(128)S(1)} %stack.106.refs_0_, s32[8]{0:T(128)S(1)} %stack.111.refs_1_, s32[8]{0:T(128)S(1)} %stack.114.refs_2_, f32[4,192]{1,0:T(4,128)S(1)} %get-tuple-element.162.refs_3_, f32[6,48,128]{2,1,0:T(8,128)S(1)} %get-tuple-element.177.refs_4_, f32[10,48,128]{2,1,0:T(8,128)S(1)} %get-tuple-element.186.refs_5_, ...), custom_call_target="tpu_custom_call" | custom-call | tf_op jit(solution)/shard_map/quad/pallas_call | solution.py:180
  167.6 14.2 %all_to_all.31 = f32[16,56,128]{2,1,0:T(8,128)S(1)} all-to-all(f32[16,56,128]{2,1,0:T(8,128)S(1)} %quad.1), channel_id=1, replica_groups=mesh['band'=16,'gvec'=16] {'gvec'}, dimensions={0} | all-to-all | bytes 917504 | tf_op jit(solution)/shard_map/all_to_all | solution.py:308
  182.6 8.2 %all-to-all-start.6 = ((f32[16,1,16]{2,1,0:T(1,128)}), f32[16,1,16]{2,1,0:T(1,128)S(1)}, u32[]{:S(2)}, u32[]{:S(2)}) async-start(f32[16,1,16]{2,1,0:T(1,128)} %broadcast_in_dim.30), calls=%async_computation.6 | async-start | bytes 16384 | tf_op jit(solution)/shard_map/all_to_all | solution.py:312
  191.6 6.3 %all-to-all-done.6 = f32[16,1,16]{2,1,0:T(1,128)S(1)} async-done(((f32[16,1,16]{2,1,0:T(1,128)}), f32[16,1,16]{2,1,0:T(1,128)S(1)}, u32[]{:S(2)}, u32[]{:S(2)}) %all-to-all-start.6) | async-done | bytes 1056 | tf_op jit(solution)/shard_map/all_to_all | solution.py:312
  (88 shorter events, 47.9 us)
Async XLA Ops:
  2.9 17.5 %collective-permute-start.22 = (bf16[3750,128]{1,0:T(8,128)(2,1)S(1)}, bf16[3750,128]{1,0:T(8,128)(2,1)S(1)}, u32[]{:S(2)}, u32[]{:S(2)}) collective-permute-start(bf16[3750,128]{1,0:T(8,128)(2,1)S(1)} %pad.3.refs_0_), channel_id=1, source_target_pairs={{0,16},{16,0},{32,48},{48,32},{64,80},{80,64},{96,112},{112,96},{1... | collective-permute-start | bytes 2880008 | tf_op jit(solution)/shard_map/cond/branch_1_fun/ppermute | solution.py:211
  6.2 24.5 %collective-permute-start.21 = (bf16[3750,128]{1,0:T(8,128)(2,1)S(1)}, bf16[3750,128]{1,0:T(8,128)(2,1)}, u32[]{:S(2)}, u32[]{:S(2)}) collective-permute-start(bf16[3750,128]{1,0:T(8,128)(2,1)S(1)} %pad.3.refs_0_), channel_id=1, source_target_pairs={{0,224},{16,240},{32,0},{48,16},{64,32},{80,48},{96,64},{112,80},{... | collective-permute-start | bytes 2880008 | tf_op jit(solution)/shard_map/cond/branch_1_fun/ppermute | solution.py:208
  10.1 23.8 %collective-permute-start.20 = (bf16[3750,128]{1,0:T(8,128)(2,1)S(1)}, bf16[3750,128]{1,0:T(8,128)(2,1)}, u32[]{:S(2)}, u32[]{:S(2)}) collective-permute-start(bf16[3750,128]{1,0:T(8,128)(2,1)S(1)} %pad.3.refs_0_), channel_id=1, source_target_pairs={{0,32},{16,48},{32,64},{48,80},{64,96},{80,112},{96,128},{112,144}... | collective-permute-start | bytes 2880008 | tf_op jit(solution)/shard_map/cond/branch_1_fun/ppermute | solution.py:208
  15.8 18.1 %collective-permute-start.23 = (bf16[2,128,2048]{2,1,0:T(8,128)(2,1)}, bf16[2,128,2048]{2,1,0:T(8,128)(2,1)}, u32[]{:S(2)}, u32[]{:S(2)}) collective-permute-start(bf16[2,128,2048]{2,1,0:T(8,128)(2,1)} %get-tuple-element.318), channel_id=1, source_target_pairs={{0,1},{1,2},{2,3},{3,0},{4,5},{5,6},{6,7},{7,4},{8,9},{9,10},{10,1... | collective-permute-start | bytes 3145736 | tf_op jit(solution)/shard_map/cond/branch_1_fun/ppermute | solution.py:222
  33.9 27.2 %collective-permute-start.4 = (bf16[2,128,2048]{2,1,0:T(8,128)(2,1)}, bf16[2,128,2048]{2,1,0:T(8,128)(2,1)}, u32[]{:S(2)}, u32[]{:S(2)}) collective-permute-start(bf16[2,128,2048]{2,1,0:T(8,128)(2,1)} %get-tuple-element.94), channel_id=1, source_target_pairs={{0,1},{1,2},{2,3},{3,0},{4,5},{5,6},{6,7},{7,4},{8,9},{9,10},{10,1... | collective-permute-start | bytes 3145736 | tf_op jit(solution)/shard_map/cond/branch_1_fun/ppermute | solution.py:222
  36.4 9.4 %collective-permute-start.2 = (bf16[3750,128]{1,0:T(8,128)(2,1)}, bf16[3750,128]{1,0:T(8,128)(2,1)S(1)}, u32[]{:S(2)}, u32[]{:S(2)}) collective-permute-start(bf16[3750,128]{1,0:T(8,128)(2,1)} %get-tuple-element.90.refs_0_), channel_id=1, source_target_pairs={{0,16},{16,0},{32,48},{48,32},{64,80},{80,64},{96,112},{112,96},{1... | collective-permute-start | bytes 2880008 | tf_op jit(solution)/shard_map/cond/branch_1_fun/ppermute | solution.py:211
  36.6 9.2 %collective-permute-start.3 = (bf16[3750,128]{1,0:T(8,128)(2,1)}, bf16[3750,128]{1,0:T(8,128)(2,1)S(1)}, u32[]{:S(2)}, u32[]{:S(2)}) collective-permute-start(bf16[3750,128]{1,0:T(8,128)(2,1)} %get-tuple-element.91.refs_2_), channel_id=1, source_target_pairs={{0,16},{16,0},{32,48},{48,32},{64,80},{80,64},{96,112},{112,96},{1... | collective-permute-start | bytes 2880008 | tf_op jit(solution)/shard_map/cond/branch_1_fun/ppermute | solution.py:211
  36.9 24.2 %collective-permute-start = (bf16[3750,128]{1,0:T(8,128)(2,1)}, bf16[3750,128]{1,0:T(8,128)(2,1)}, u32[]{:S(2)}, u32[]{:S(2)}) collective-permute-start(bf16[3750,128]{1,0:T(8,128)(2,1)} %get-tuple-element.90.refs_0_), channel_id=1, source_target_pairs={{0,32},{16,48},{32,64},{48,80},{64,96},{80,112},{96,128},{112,144}... | collective-permute-start | bytes 2880008 | tf_op jit(solution)/shard_map/cond/branch_1_fun/ppermute | solution.py:208
  36.9 24.2 %collective-permute-start.1 = (bf16[3750,128]{1,0:T(8,128)(2,1)}, bf16[3750,128]{1,0:T(8,128)(2,1)}, u32[]{:S(2)}, u32[]{:S(2)}) collective-permute-start(bf16[3750,128]{1,0:T(8,128)(2,1)} %get-tuple-element.91.refs_2_), channel_id=1, source_target_pairs={{0,224},{16,240},{32,0},{48,16},{64,32},{80,48},{96,64},{112,80},{... | collective-permute-start | bytes 2880008 | tf_op jit(solution)/shard_map/cond/branch_1_fun/ppermute | solution.py:208
  39.6 16.7 %all-to-all-start = ((s16[16,48,256]{2,1,0:T(8,128)(2,1)}), s16[16,48,256]{2,1,0:T(8,128)(2,1)}, u32[]{:S(2)}, u32[]{:S(2)}) async-start(s16[16,48,256]{2,1,0:T(8,128)(2,1)} %get-tuple-element.93), calls=%async_computation | async-start | bytes 786432 | tf_op jit(solution)/shard_map/cond/branch_1_fun/all_to_all | solution.py:260
  61.3 26.1 %collective-permute-start.9 = (bf16[2,128,2048]{2,1,0:T(8,128)(2,1)S(1)}, bf16[2,128,2048]{2,1,0:T(8,128)(2,1)}, u32[]{:S(2)}, u32[]{:S(2)}) collective-permute-start(bf16[2,128,2048]{2,1,0:T(8,128)(2,1)S(1)} %get-tuple-element.99), channel_id=1, source_target_pairs={{0,1},{1,2},{2,3},{3,0},{4,5},{5,6},{6,7},{7,4},{8,9},{9,10},{10,1... | collective-permute-start | bytes 3145736 | tf_op jit(solution)/shard_map/cond/branch_1_fun/ppermute | solution.py:222
  62.2 9.9 %collective-permute-start.7 = (bf16[3750,128]{1,0:T(8,128)(2,1)}, bf16[3750,128]{1,0:T(8,128)(2,1)S(1)}, u32[]{:S(2)}, u32[]{:S(2)}) collective-permute-start(bf16[3750,128]{1,0:T(8,128)(2,1)} %get-tuple-element.95.refs_0_), channel_id=1, source_target_pairs={{0,16},{16,0},{32,48},{48,32},{64,80},{80,64},{96,112},{112,96},{1... | collective-permute-start | bytes 2880008 | tf_op jit(solution)/shard_map/cond/branch_1_fun/ppermute | solution.py:211
  63.6 8.5 %collective-permute-start.8 = (bf16[3750,128]{1,0:T(8,128)(2,1)}, bf16[3750,128]{1,0:T(8,128)(2,1)S(1)}, u32[]{:S(2)}, u32[]{:S(2)}) collective-permute-start(bf16[3750,128]{1,0:T(8,128)(2,1)} %get-tuple-element.96.refs_2_), channel_id=1, source_target_pairs={{0,16},{16,0},{32,48},{48,32},{64,80},{80,64},{96,112},{112,96},{1... | collective-permute-start | bytes 2880008 | tf_op jit(solution)/shard_map/cond/branch_1_fun/ppermute | solution.py:211
  63.6 23.9 %collective-permute-start.5 = (bf16[3750,128]{1,0:T(8,128)(2,1)}, bf16[3750,128]{1,0:T(8,128)(2,1)}, u32[]{:S(2)}, u32[]{:S(2)}) collective-permute-start(bf16[3750,128]{1,0:T(8,128)(2,1)} %get-tuple-element.95.refs_0_), channel_id=1, source_target_pairs={{0,32},{16,48},{32,64},{48,80},{64,96},{80,112},{96,128},{112,144}... | collective-permute-start | bytes 2880008 | tf_op jit(solution)/shard_map/cond/branch_1_fun/ppermute | solution.py:208
  63.6 23.9 %collective-permute-start.6 = (bf16[3750,128]{1,0:T(8,128)(2,1)}, bf16[3750,128]{1,0:T(8,128)(2,1)}, u32[]{:S(2)}, u32[]{:S(2)}) collective-permute-start(bf16[3750,128]{1,0:T(8,128)(2,1)} %get-tuple-element.96.refs_2_), channel_id=1, source_target_pairs={{0,224},{16,240},{32,0},{48,16},{64,32},{80,48},{96,64},{112,80},{... | collective-permute-start | bytes 2880008 | tf_op jit(solution)/shard_map/cond/branch_1_fun/ppermute | solution.py:208
  66.3 20.8 %all-to-all-start.1 = ((s16[16,48,512]{2,1,0:T(8,128)(2,1)}), s16[16,48,512]{2,1,0:T(8,128)(2,1)}, u32[]{:S(2)}, u32[]{:S(2)}) async-start(s16[16,48,512]{2,1,0:T(8,128)(2,1)} %get-tuple-element.98), calls=%async_computation.1 | async-start | bytes 1572864 | tf_op jit(solution)/shard_map/cond/branch_1_fun/all_to_all | solution.py:260
  87.5 13.3 %collective-permute-start.26 = (bf16[3750,128]{1,0:T(8,128)(2,1)}, bf16[3750,128]{1,0:T(8,128)(2,1)S(1)}, u32[]{:S(2)}, u32[]{:S(2)}) collective-permute-start(bf16[3750,128]{1,0:T(8,128)(2,1)} %get-tuple-element.102.refs_2_), channel_id=1, source_target_pairs={{0,16},{16,0},{32,48},{48,32},{64,80},{80,64},{96,112},{112,96},{1... | collective-permute-start | bytes 2880008 | tf_op jit(solution)/shard_map/cond/branch_1_fun/ppermute | solution.py:211
  89.3 11.4 %collective-permute-start.25 = (bf16[3750,128]{1,0:T(8,128)(2,1)}, bf16[3750,128]{1,0:T(8,128)(2,1)S(1)}, u32[]{:S(2)}, u32[]{:S(2)}) collective-permute-start(bf16[3750,128]{1,0:T(8,128)(2,1)} %get-tuple-element.101.refs_0_), channel_id=1, source_target_pairs={{0,16},{16,0},{32,48},{48,32},{64,80},{80,64},{96,112},{112,96},{1... | collective-permute-start | bytes 2880008 | tf_op jit(solution)/shard_map/cond/branch_1_fun/ppermute | solution.py:211
  90.8 21.5 %collective-permute-start.24 = (bf16[3750,128]{1,0:T(8,128)(2,1)S(1)}, bf16[3750,128]{1,0:T(8,128)(2,1)}, u32[]{:S(2)}, u32[]{:S(2)}) collective-permute-start(bf16[3750,128]{1,0:T(8,128)(2,1)S(1)} %broadcast_select_fusion), channel_id=1, source_target_pairs={{0,32},{16,240},{32,64},{48,16},{64,96},{80,48},{96,128},{112,80},... | collective-permute-start | bytes 2880008 | tf_op jit(solution)/shard_map/cond/branch_1_fun/ppermute | solution.py:225
  93.4 18.9 %all-to-all-start.4 = ((s16[16,48,512]{2,1,0:T(8,128)(2,1)}), s16[16,48,512]{2,1,0:T(8,128)(2,1)}, u32[]{:S(2)}, u32[]{:S(2)}) async-start(s16[16,48,512]{2,1,0:T(8,128)(2,1)} %get-tuple-element.104), calls=%async_computation.4 | async-start | bytes 1572864 | tf_op jit(solution)/shard_map/cond/branch_1_fun/all_to_all | solution.py:260
  112.4 18.0 %all-to-all-start.3 = ((s16[16,48,512]{2,1,0:T(8,128)(2,1)}), s16[16,48,512]{2,1,0:T(8,128)(2,1)}, u32[]{:S(2)}, u32[]{:S(2)}) async-start(s16[16,48,512]{2,1,0:T(8,128)(2,1)} %get-tuple-element.112), calls=%async_computation.3 | async-start | bytes 1572864 | tf_op jit(solution)/shard_map/cond/branch_1_fun/all_to_all | solution.py:260
  116.7 30.5 %collective-permute-start.14 = (bf16[2,128,2048]{2,1,0:T(8,128)(2,1)}, bf16[2,128,2048]{2,1,0:T(8,128)(2,1)}, u32[]{:S(2)}, u32[]{:S(2)}) collective-permute-start(bf16[2,128,2048]{2,1,0:T(8,128)(2,1)} %get-tuple-element.114), channel_id=1, source_target_pairs={{0,16},{16,0},{32,48},{48,32},{64,80},{80,64},{96,112},{112,96},{1... | collective-permute-start | bytes 3145736 | tf_op jit(solution)/shard_map/cond/branch_1_fun/ppermute | solution.py:211
  117.3 29.9 %collective-permute-start.15 = (bf16[2,128,2048]{2,1,0:T(8,128)(2,1)}, bf16[2,128,2048]{2,1,0:T(8,128)(2,1)}, u32[]{:S(2)}, u32[]{:S(2)}) collective-permute-start(bf16[2,128,2048]{2,1,0:T(8,128)(2,1)} %get-tuple-element.115), channel_id=1, source_target_pairs={{0,16},{16,0},{32,48},{48,32},{64,80},{80,64},{96,112},{112,96},{1... | collective-permute-start | bytes 3145736 | tf_op jit(solution)/shard_map/cond/branch_1_fun/ppermute | solution.py:211
  130.3 16.8 %all-to-all-start.2 = ((s16[16,48,256]{2,1,0:T(8,128)(2,1)}), s16[16,48,256]{2,1,0:T(8,128)(2,1)}, u32[]{:S(2)}, u32[]{:S(2)}) async-start(s16[16,48,256]{2,1,0:T(8,128)(2,1)} %project.9), calls=%async_computation.2 | async-start | bytes 786432 | tf_op jit(solution)/shard_map/cond/branch_1_fun/all_to_all | solution.py:260
  134.6 7.8 %collective-permute-start.13 = (bf16[6,48,128]{2,1,0:T(8,128)(2,1)S(1)}, bf16[6,48,128]{2,1,0:T(8,128)(2,1)}, u32[]{:S(2)}, u32[]{:S(2)}) collective-permute-start(bf16[6,48,128]{2,1,0:T(8,128)(2,1)S(1)} %get-tuple-element.363), channel_id=1, source_target_pairs={{0,12},{1,13},{2,14},{3,15},{4,0},{5,1},{6,2},{7,3},{8,4},{9,5},{1... | collective-permute-start | bytes 221192 | tf_op jit(solution)/shard_map/cond/branch_1_fun/ppermute | solution.py:214
  137.1 7.9 %collective-permute-start.12 = (bf16[6,48,128]{2,1,0:T(8,128)(2,1)S(1)}, bf16[6,48,128]{2,1,0:T(8,128)(2,1)}, u32[]{:S(2)}, u32[]{:S(2)}) collective-permute-start(bf16[6,48,128]{2,1,0:T(8,128)(2,1)S(1)} %get-tuple-element.363), channel_id=1, source_target_pairs={{0,8},{1,9},{2,10},{3,11},{4,12},{5,13},{6,14},{7,15},{8,0},{9,1},... | collective-permute-start | bytes 221192 | tf_op jit(solution)/shard_map/cond/branch_1_fun/ppermute | solution.py:214
  137.6 9.6 %collective-permute-start.11 = (bf16[6,48,128]{2,1,0:T(8,128)(2,1)S(1)}, bf16[6,48,128]{2,1,0:T(8,128)(2,1)}, u32[]{:S(2)}, u32[]{:S(2)}) collective-permute-start(bf16[6,48,128]{2,1,0:T(8,128)(2,1)S(1)} %get-tuple-element.363), channel_id=1, source_target_pairs={{0,4},{1,5},{2,6},{3,7},{4,8},{5,9},{6,10},{7,11},{8,12},{9,13},{1... | collective-permute-start | bytes 221192 | tf_op jit(solution)/shard_map/cond/branch_1_fun/ppermute | solution.py:214
  147.4 13.7 %collective-permute-start.19 = (bf16[2,128,2048]{2,1,0:T(8,128)(2,1)}, bf16[2,128,2048]{2,1,0:T(8,128)(2,1)}, u32[]{:S(2)}, u32[]{:S(2)}) collective-permute-start(bf16[2,128,2048]{2,1,0:T(8,128)(2,1)} %get-tuple-element.122), channel_id=1, source_target_pairs={{0,16},{16,0},{32,48},{48,32},{64,80},{80,64},{96,112},{112,96},{1... | collective-permute-start | bytes 3145736 | tf_op jit(solution)/shard_map/cond/branch_1_fun/ppermute | solution.py:211
  150.9 5.3 %collective-permute-start.18 = (bf16[10,48,128]{2,1,0:T(8,128)(2,1)}, bf16[10,48,128]{2,1,0:T(8,128)(2,1)}, u32[]{:S(2)}, u32[]{:S(2)}) collective-permute-start(bf16[10,48,128]{2,1,0:T(8,128)(2,1)} %get-tuple-element.376), channel_id=1, source_target_pairs={{0,12},{1,13},{2,14},{3,15},{4,0},{5,1},{6,2},{7,3},{8,4},{9,5},{1... | collective-permute-start | bytes 368648 | tf_op jit(solution)/shard_map/cond/branch_1_fun/ppermute | solution.py:214
  151.4 6.4 %collective-permute-start.17 = (bf16[10,48,128]{2,1,0:T(8,128)(2,1)}, bf16[10,48,128]{2,1,0:T(8,128)(2,1)}, u32[]{:S(2)}, u32[]{:S(2)}) collective-permute-start(bf16[10,48,128]{2,1,0:T(8,128)(2,1)} %get-tuple-element.376), channel_id=1, source_target_pairs={{0,8},{1,9},{2,10},{3,11},{4,12},{5,13},{6,14},{7,15},{8,0},{9,1},... | collective-permute-start | bytes 368648 | tf_op jit(solution)/shard_map/cond/branch_1_fun/ppermute | solution.py:214
  152.0 9.1 %collective-permute-start.16 = (bf16[10,48,128]{2,1,0:T(8,128)(2,1)}, bf16[10,48,128]{2,1,0:T(8,128)(2,1)}, u32[]{:S(2)}, u32[]{:S(2)}) collective-permute-start(bf16[10,48,128]{2,1,0:T(8,128)(2,1)} %get-tuple-element.376), channel_id=1, source_target_pairs={{0,4},{1,5},{2,6},{3,7},{4,8},{5,9},{6,10},{7,11},{8,12},{9,13},{1... | collective-permute-start | bytes 368648 | tf_op jit(solution)/shard_map/cond/branch_1_fun/ppermute | solution.py:214
  182.6 15.2 %all-to-all-start.6 = ((f32[16,1,16]{2,1,0:T(1,128)}), f32[16,1,16]{2,1,0:T(1,128)S(1)}, u32[]{:S(2)}, u32[]{:S(2)}) async-start(f32[16,1,16]{2,1,0:T(1,128)} %broadcast_in_dim.30), calls=%async_computation.6 | async-start | bytes 16384 | tf_op jit(solution)/shard_map/all_to_all | solution.py:312
  (4 other events, 47.6 us)
where the time goes:
time: 200 us; the launch traced here: 198 us
  starting transfers between devices  65.5 us (33%)
  waiting for transfers between devices  55.3 us (28%)
  Pallas kernels  51.1 us (26%)
  blocking collectives  14.2 us (7%)
  local copies, waits for them, and re-layouts  6.64 us (3%)
  other arithmetic  3.58 us (2%)
    pallas_call x5, Pallas kernels, project(): pl.pallas_call(lambda pd_ref, *refs: project_kernel(shape, pd_ref, *refs[...  37.4 us
    all_to_all x5, starting transfers between devices, send(): return lax.all_to_all(code, 'gvec', 0, 0)  26.1 us
    all_to_all x5, waiting for transfers between devices, send(): return lax.all_to_all(code, 'gvec', 0, 0)  19 us
    ppermute x6, waiting for transfers between devices, along_y(): lax.ppermute(value, 'gvec', [(g, (g + SIDE * by) % devices) for g in rang...  17.6 us
    all_to_all x1, blocking collectives, local(): landed = lax.all_to_all(message, 'gvec', 0, 0)  14.2 us
    ppermute x6, waiting for transfers between devices, shift(): lax.ppermute(value, 'band', [(b, (b + 2 * by) % bands) for b in range(ban...  12.4 us
    ppermute x6, starting transfers between devices, shift(): lax.ppermute(value, 'band', [(b, (b + 2 * by) % bands) for b in range(ban...  9.21 us
    ppermute x11, starting transfers between devices, sibling(): return lax.ppermute(value, 'band', [(b, b ^ 1) for b in range(bands)])  8.5 us
  transfers between devices with their start and end apart: 33, of which 15 were waited for; matrix products, arithmetic and copies ran while one was open for 4% of the time, Pallas kernels for 23%

commit v1 on v0

--- a/solution.py
+++ b/solution.py
@@ -74,51 +74,61 @@
     out_ref[...] = code.reshape(out_ref.shape)
 
 
-def project(flat, blocks, devices, ahead=()):
+def project(flat, blocks, devices, room=0, into=None):
     nrows, depth = flat.shape
     share = nrows // devices
     shape = [len(block) for block in blocks]
     parts = [part for block in blocks for part in block]
     width = len(blocks) * LANES
+    whole = width + room * LANES if into is None else into.shape[2]
+    place = 0 if into is None else whole // width - 1
+    extra = () if into is None else (into,)
     return pl.pallas_call(
         lambda pd_ref, *refs: project_kernel(shape, pd_ref, *refs[: len(parts)], refs[-1]),
         grid=(SPLIT,),
         in_specs=[pl.BlockSpec((nrows // SPLIT, depth), lambda i: (i, 0))]
         + [pl.BlockSpec(part.shape, lambda i: (0, 0)) for part in parts]
-        + [ANYWHERE] * len(ahead),
-        out_specs=pl.BlockSpec((devices // SPLIT, share, width), lambda i: (i, 0, 0)),
-        out_shape=pltpu.HBM((devices, share, width), jnp.int16),
+        + [ANYWHERE] * len(extra),
+        out_specs=pl.BlockSpec((devices // SPLIT, share, width), lambda i: (i, 0, place)),
+        out_shape=pltpu.HBM((devices, share, whole), jnp.int16),
+        input_output_aliases={1 + len(parts): 0} if extra else {},
         compiler_params=pltpu.CompilerParams(vmem_limit_bytes=32 * MEGA),
         cost_estimate=pl.CostEstimate(flops=10**6, bytes_accessed=10**4, transcendentals=0),
         name="project",
-    )(pin(flat), *parts, *ahead)
-
-
-def collect_kernel(count, live_ref, *refs):
-    codes, coef_ref, rounded_ref = refs[:count], refs[count], refs[count + 1]
-    at = 0
-    for code_ref in codes:
+    )(pin(flat), *parts, *map(pin, extra))
+
+
+def collect_kernel(cuts, kept, live_ref, *refs):
+    codes, before, coef_ref, rounded_ref = refs[: len(cuts)], refs[len(cuts) : -2], refs[-2], refs[-1]
+    at = kept
+    if kept:
+        coef_ref[0:kept] = before[0][...]
+        rounded_ref[0:kept] = before[1][...]
+    for code_ref, cut in zip(codes, cuts):
         devices, rows, width = code_ref.shape
-        total = jnp.zeros((rows, width), jnp.float32)
-        for d in range(devices):
-            power = code_ref[d, :, 0:LANES].astype(jnp.int32)[:, LANES - 1 : LANES]
-            unit = 1.0 / (jnp.ones_like(power) << power).astype(jnp.float32)
-            total += code_ref[d].astype(jnp.int32).astype(jnp.float32) * unit
-        lane = lax.broadcasted_iota(jnp.int32, total.shape, 1)
-        total = jnp.where(lane == LANES - 1, 0.0, total) * live_ref[...]
-        for n in range(width // LANES):
-            part = total[:, n * LANES : (n + 1) * LANES]
-            coef_ref[at] = part
-            rounded_ref[at] = part.astype(jnp.bfloat16)
-            at += 1
-
-
-def collect(codes, live_rows, ahead=()):
+        for begin, end in zip((0, *cut), (*cut, width)):
+            total = jnp.zeros((rows, end - begin), jnp.float32)
+            for d in range(devices):
+                power = code_ref[d, :, begin : begin + LANES].astype(jnp.int32)[:, LANES - 1 : LANES]
+                unit = 1.0 / (jnp.ones_like(power) << power).astype(jnp.float32)
+                total += code_ref[d, :, begin:end].astype(jnp.int32).astype(jnp.float32) * unit
+            lane = lax.broadcasted_iota(jnp.int32, total.shape, 1)
+            total = jnp.where(lane == LANES - 1, 0.0, total) * live_ref[...]
+            for n in range((end - begin) // LANES):
+                part = total[:, n * LANES : (n + 1) * LANES]
+                coef_ref[at] = part
+                rounded_ref[at] = part.astype(jnp.bfloat16)
+                at += 1
+
+
+def collect(codes, live_rows, cuts=None, before=()):
     rows = codes[0].shape[1]
-    total = sum(code.shape[2] // LANES for code in codes)
+    kept = before[0].shape[0] if before else 0
+    total = kept + sum(code.shape[2] // LANES for code in codes)
+    cuts = cuts or [()] * len(codes)
     return pl.pallas_call(
-        lambda *refs: collect_kernel(len(codes), *refs[: 1 + len(codes)], *refs[-2:]),
-        in_specs=[IN_VMEM] * (1 + len(codes)) + [ANYWHERE] * len(ahead),
+        lambda *refs: collect_kernel(cuts, kept, *refs),
+        in_specs=[IN_VMEM] * (1 + len(codes) + len(before)),
         out_specs=(IN_VMEM, IN_VMEM),
         out_shape=(
             jax.ShapeDtypeStruct((total, rows, LANES), jnp.float32),
@@ -126,7 +136,7 @@
         ),
         compiler_params=pltpu.CompilerParams(vmem_limit_bytes=12 * MEGA),
         name="collect",
-    )(live_rows, *codes, *ahead)
+    )(live_rows, *codes, *before)
 
 
 def quad_kernel(groups, tables, ids_ref, own_ref, node_ref, pick_ref, *refs):
@@ -286,23 +296,25 @@
     def fourth(flat, up, down, code, landing, live_here):
         far = along_z(jnp.where(core == 0, up, down))
         coef, rounded = collect(landing, live_here)
-        return far, project(flat, pair_up([(up,), (down,)]), devices), send(code), coef, rounded
-
-    def fifth(flat, far, code, rounded, near, farther):
-        swapped = [sibling(near), sibling(farther)]
-        return send(project(flat, pair_up([(far,)]), devices)), send(code), spread_rows(rounded), swapped
-
-    def sixth(landing, live_here, across):
-        coef, rounded = collect(landing, live_here)
-        return coef, spread_rows(rounded), sibling(across)
+        code_now = project(flat, pair_up([(up,), (down,)]), devices, room=2)
+        return far, code_now, send(code), coef, spread_rows(rounded)
+
+    def fifth(flat, far, code, landing, live_here, near, farther, across):
+        swapped = [sibling(near), sibling(farther), sibling(across)]
+        code = project(flat, pair_up([(far,)]), devices, into=code)
+        return send(code), collect(landing, live_here), swapped
+
+    def sixth(landing, live_here, before):
+        coef, rounded = collect(landing, live_here, [(4 * LANES,)], before)
+        return coef, spread_rows(rounded)
 
     up, down, code, table, near, pick, live_here = window(first, flat, eigvecs, subspace, band_weight, freq_index)
     up, down, code, landed_0, across = window(middle, flat, up, down, code, near)
     up, down, code, landed_1, farther = window(middle, flat, up, down, code, table[1])
-    far, code, landed_2, coef_a, rounded = window(fourth, flat, up, down, code, [landed_0, landed_1], live_here)
-    landed_4, landed_3, pieces_a, swapped = window(fifth, flat, far, code, rounded, near, farther)
-    coef_b, pieces_b, across_swapped = window(sixth, [landed_2, landed_3, landed_4], live_here, across)
-    weights = [*table, near, farther, *swapped, across, across_swapped]
+    far, code, landed_2, coef_a, pieces_a = window(fourth, flat, up, down, code, [landed_0, landed_1], live_here)
+    landed_3, before, swapped = window(fifth, flat, far, code, [landed_2], live_here, near, farther, across)
+    coef_b, pieces_b = window(sixth, [landed_3], live_here, before)
+    weights = [*table, near, farther, swapped[0], swapped[1], across, swapped[2]]
     coefs, pieces = [coef_a, coef_b], pieces_a + pieces_b
     message = quadratic(ids, own, nodes_at, pick, coefs, pieces, weights)
     landed = lax.all_to_all(message, "gvec", 0, 0)

time: 200 us -> 196 us (0.980)
  starting transfers between devices: 65.5 us -> 60.3 us
  blocking collectives: 14.2 us -> 16.7 us
    ppermute x6, waiting for transfers between devices: 17.6 us -> 6.68 us  [along_y(): lax.ppermute(value, 'gvec', [(g, (g + SIDE * by) % devices) for g in rang...]
    ppermute x11, waiting for transfers between devices: 0.03 us -> 6.02 us  [sibling(): return lax.ppermute(value, 'band', [(b, b ^ 1) for b in range(bands)])]
    all_to_all x5 -> x4, starting transfers between devices: 26.1 us -> 22.8 us  [send(): return lax.all_to_all(code, 'gvec', 0, 0)]
    all_to_all x5 -> x4, waiting for transfers between devices: 19 us -> 22 us  [send(): return lax.all_to_all(code, 'gvec', 0, 0)]
    all_to_all x1, blocking collectives: 14.2 us -> 16.7 us  [local(): landed = lax.all_to_all(message, 'gvec', 0, 0)]
    all_to_all x1, starting transfers between devices: 8.19 us -> 6.02 us  [local(): lax.all_to_all(jnp.broadcast_to(terms, (bands, states)), 'band', 0, 0)]
    pallas_call x2 -> x3, Pallas kernels: 4.46 us -> 6.03 us  [collect(): pl.pallas_call(lambda *refs: collect_kernel(cuts, kept, *refs), in_specs=...]
  transfers between devices with their start and end apart: 33 -> 32, of which waited for: 15 -> 16; matrix products, arithmetic and copies ran while one was open for 4% -> 4% of each run, Pallas kernels for 23% -> 19%
where the time goes in v1:
time: 196 us; the launch traced here: 195 us
  starting transfers between devices  60.3 us (31%)
  waiting for transfers between devices  53.4 us (27%)
  Pallas kernels  52.7 us (27%)
  blocking collectives  16.7 us (9%)
  local copies, waits for them, and re-layouts  6.69 us (3%)
  other arithmetic  3.58 us (2%)
    pallas_call x5, Pallas kernels, project(): pl.pallas_call(lambda pd_ref, *refs: project_kernel(shape, pd_ref, *refs[...  37.4 us
    all_to_all x4, starting transfers between devices, send(): return lax.all_to_all(code, 'gvec', 0, 0)  22.8 us
    all_to_all x4, waiting for transfers between devices, send(): return lax.all_to_all(code, 'gvec', 0, 0)  22 us
    all_to_all x1, blocking collectives, local(): landed = lax.all_to_all(message, 'gvec', 0, 0)  16.7 us
    ppermute x6, waiting for transfers between devices, shift(): lax.ppermute(value, 'band', [(b, (b + 2 * by) % bands) for b in range(ban...  12.4 us
    ppermute x6, starting transfers between devices, shift(): lax.ppermute(value, 'band', [(b, (b + 2 * by) % bands) for b in range(ban...  9.21 us
    ppermute x11, starting transfers between devices, sibling(): return lax.ppermute(value, 'band', [(b, b ^ 1) for b in range(bands)])  8.67 us
    ppermute x6, waiting for transfers between devices, along_y(): lax.ppermute(value, 'gvec', [(g, (g + SIDE * by) % devices) for g in rang...  6.68 us
  transfers between devices with their start and end apart: 32, of which 16 were waited for; matrix products, arithmetic and copies ran while one was open for 4% of the time, Pallas kernels for 19%

profile of v1, /device:TPU:1, one launch (start us, length us, event | category | flops | bytes accessed | tf_op | source)
XLA Modules:
  0.0 195.1 jit_solution(1225703991541869936)
XLA Ops:
  1.5 32.4 %conditional.6 = (bf16[3750,128]{1,0:T(8,128)(2,1)}, bf16[3750,128]{1,0:T(8,128)(2,1)}, s16[16,48,256]{2,1,0:T(8,128)(2,1)}, bf16[2,128,2048]{2,1,0:T(8,128)(2,1...) conditional(s32[]{:T(128)} %bitcast.32, () %tuple.56, ...), branch_computations={%region_0.0_spmd, %region_1.2_spmd} | conditional | flops 1003006 | bytes 21678728 | solution.py:259
  2.9 3.3 %collective-permute-start.19 = (bf16[3750,128]{1,0:T(8,128)(2,1)S(1)}, bf16[3750,128]{1,0:T(8,128)(2,1)S(1)}, u32[]{:S(2)}, u32[]{:S(2)}) collective-permute-start(bf16[3750,128]{1,0:T(8,128)(2,1)S(1)} %pad.3.refs_0_), channel_id=1, source_target_pairs={{0,16},{16,0},{32,48},{48,32},{64,80},{80,64},{96,112},{112,96},{1... | collective-permute-start | bytes 2880008 | tf_op jit(solution)/shard_map/cond/branch_1_fun/ppermute | solution.py:221
  6.2 3.9 %collective-permute-start.18 = (bf16[3750,128]{1,0:T(8,128)(2,1)S(1)}, bf16[3750,128]{1,0:T(8,128)(2,1)}, u32[]{:S(2)}, u32[]{:S(2)}) collective-permute-start(bf16[3750,128]{1,0:T(8,128)(2,1)S(1)} %pad.3.refs_0_), channel_id=1, source_target_pairs={{0,224},{16,240},{32,0},{48,16},{64,32},{80,48},{96,64},{112,80},{... | collective-permute-start | bytes 2880008 | tf_op jit(solution)/shard_map/cond/branch_1_fun/ppermute | solution.py:218
  10.1 2.7 %copy.28.w_ref = bf16[4,125,2000]{2,1,0:T(8,128)(2,1)S(1)} copy(bf16[4,125,2000]{2,0,1:T(4,128)(2,1)} %get-tuple-element.305) | data formatting | bytes 4000000 | tf_op jit(solution)/shard_map
  12.8 2.9 %spread.1 = (bf16[2,128,2048]{2,1,0:T(8,128)(2,1)}, bf16[2,128,2048]{2,1,0:T(8,128)(2,1)S(1)}) custom-call(s32[2]{0:T(128)S(1)} %get-tuple-element.82.first_ref, bf16[4,125,2000]{2,1,0:T(8,128)(2,1)S(1)} %copy.28.w_ref), custom_call_target="tpu_custom_call" | custom-call | tf_op jit(solution)/shard_map/cond/branch_1_fun/spread/pallas_call | solution.py:46
  20.4 6.4 %project.5 = s16[16,48,256]{2,1,0:T(8,128)(2,1)} custom-call(bf16[768,3750]{1,0:T(8,128)(2,1)} %get-tuple-element.81.pd_ref, bf16[3750,128]{1,0:T(8,128)(2,1)S(1)} %pad.3.refs_0_, bf16[3750,128]{1,0:T(8,128)(2,1)S(1)} %collective-permute-done.19.refs_1_), custom_call_target="tpu_custom_call" | custom-call | flops 1000000 | bytes 10000 | tf_op jit(solution)/shard_map/cond/branch_1_fun/project/pallas_call | solution.py:86
  26.7 4.0 %collective-permute-done.18 = bf16[3750,128]{1,0:T(8,128)(2,1)} collective-permute-done((bf16[3750,128]{1,0:T(8,128)(2,1)S(1)}, bf16[3750,128]{1,0:T(8,128)(2,1)}, u32[]{:S(2)}, u32[]{:S(2)}) %collective-permute-start.18) | collective-permute-done | bytes 960032 | tf_op jit(solution)/shard_map/cond/branch_1_fun/ppermute | solution.py:218
  30.7 3.2 %collective-permute-done.17 = bf16[3750,128]{1,0:T(8,128)(2,1)} collective-permute-done((bf16[3750,128]{1,0:T(8,128)(2,1)S(1)}, bf16[3750,128]{1,0:T(8,128)(2,1)}, u32[]{:S(2)}, u32[]{:S(2)}) %collective-permute-start.17) | collective-permute-done | bytes 960032 | tf_op jit(solution)/shard_map/cond/branch_1_fun/ppermute | solution.py:218
  33.9 27.2 %conditional.7 = (bf16[3750,128]{1,0:T(8,128)(2,1)}, bf16[3750,128]{1,0:T(8,128)(2,1)}, s16[16,48,512]{2,1,0:T(8,128)(2,1)}, s16[16,48,256]{2,1,0:T(8,128)(2,1)}, bf16[2,128,2048]{2,1,0:T(8,128)(2,1)}) conditional(s32[]{:T(128)} %bitcast.32, () %tuple.60, (bf16[3750,128]{1,0:T(8,128)(2,1)}, bf16[3750,128]{1,0:T(8,128)(2,1)}, ...), branch_computations={%region_2.3_spmd, %region_3.4_spmd} | conditional | flops 1000000 | bytes 20744224 | solution.py:259
  36.9 2.7 %collective-permute-start.1 = (bf16[3750,128]{1,0:T(8,128)(2,1)}, bf16[3750,128]{1,0:T(8,128)(2,1)}, u32[]{:S(2)}, u32[]{:S(2)}) collective-permute-start(bf16[3750,128]{1,0:T(8,128)(2,1)} %get-tuple-element.93.refs_2_), channel_id=1, source_target_pairs={{0,224},{16,240},{32,0},{48,16},{64,32},{80,48},{96,64},{112,80},{... | collective-permute-start | bytes 2880008 | tf_op jit(solution)/shard_map/cond/branch_1_fun/ppermute | solution.py:218
  39.6 6.2 %all-to-all-start = ((s16[16,48,256]{2,1,0:T(8,128)(2,1)}), s16[16,48,256]{2,1,0:T(8,128)(2,1)}, u32[]{:S(2)}, u32[]{:S(2)}) async-start(s16[16,48,256]{2,1,0:T(8,128)(2,1)} %get-tuple-element.95), calls=%async_computation | async-start | bytes 786432 | tf_op jit(solution)/shard_map/cond/branch_1_fun/all_to_all | solution.py:270
  45.8 8.1 %project.6 = s16[16,48,512]{2,1,0:T(8,128)(2,1)} custom-call(bf16[768,3750]{1,0:T(8,128)(2,1)} %get-tuple-element.94.pd_ref, bf16[3750,128]{1,0:T(8,128)(2,1)} %get-tuple-element.92.refs_0_, bf16[3750,128]{1,0:T(8,128)(2,1)S(1)} %collective-permute-done.2.refs_1_, bf16[3750,128]{1,0:T(8,128)(2,1)} %get-tuple-element.93.refs_2_, ...), custom_call_target="tpu_custom_call" | custom-call | flops 1000000 | bytes 10000 | tf_op jit(solution)/shard_map/cond/branch_1_fun/project/pallas_call | solution.py:86
  56.3 4.9 %collective-permute-done = bf16[3750,128]{1,0:T(8,128)(2,1)} collective-permute-done((bf16[3750,128]{1,0:T(8,128)(2,1)}, bf16[3750,128]{1,0:T(8,128)(2,1)}, u32[]{:S(2)}, u32[]{:S(2)}) %collective-permute-start) | collective-permute-done | bytes 960032 | tf_op jit(solution)/shard_map/cond/branch_1_fun/ppermute | solution.py:218
  61.1 26.3 %conditional.8 = (bf16[3750,128]{1,0:T(8,128)(2,1)}, bf16[3750,128]{1,0:T(8,128)(2,1)}, s16[16,48,512]{2,1,0:T(8,128)(2,1)}, s16[16,48,512]{2,1,0:T(8,128)(2,1)}, bf16[2,128,2048]{2,1,0:T(8,128)(2,1)}) conditional(s32[]{:T(128)} %bitcast.32, () %tuple.59, (bf16[3750,128]{1,0:T(8,128)(2,1)}, bf16[3750,128]{1,0:T(8,128)(2,1)}, ...), branch_computations={%region_4.5_spmd, %region_5.6_spmd} | conditional | flops 1000000 | bytes 21923872 | solution.py:259
  63.6 2.7 %collective-permute-start.6 = (bf16[3750,128]{1,0:T(8,128)(2,1)}, bf16[3750,128]{1,0:T(8,128)(2,1)}, u32[]{:S(2)}, u32[]{:S(2)}) collective-permute-start(bf16[3750,128]{1,0:T(8,128)(2,1)} %get-tuple-element.98.refs_2_), channel_id=1, source_target_pairs={{0,224},{16,240},{32,0},{48,16},{64,32},{80,48},{96,64},{112,80},{... | collective-permute-start | bytes 2880008 | tf_op jit(solution)/shard_map/cond/branch_1_fun/ppermute | solution.py:218
  66.3 5.8 %all-to-all-start.1 = ((s16[16,48,512]{2,1,0:T(8,128)(2,1)}), s16[16,48,512]{2,1,0:T(8,128)(2,1)}, u32[]{:S(2)}, u32[]{:S(2)}) async-start(s16[16,48,512]{2,1,0:T(8,128)(2,1)} %get-tuple-element.100), calls=%async_computation.1 | async-start | bytes 1572864 | tf_op jit(solution)/shard_map/cond/branch_1_fun/all_to_all | solution.py:270
  72.1 8.1 %project.7 = s16[16,48,512]{2,1,0:T(8,128)(2,1)} custom-call(bf16[768,3750]{1,0:T(8,128)(2,1)} %get-tuple-element.99.pd_ref, bf16[3750,128]{1,0:T(8,128)(2,1)} %get-tuple-element.97.refs_0_, bf16[3750,128]{1,0:T(8,128)(2,1)S(1)} %collective-permute-done.7.refs_1_, bf16[3750,128]{1,0:T(8,128)(2,1)} %get-tuple-element.98.refs_2_, ...), custom_call_target="tpu_custom_call" | custom-call | flops 1000000 | bytes 10000 | tf_op jit(solution)/shard_map/cond/branch_1_fun/project/pallas_call | solution.py:86
  80.3 6.8 %all-to-all-done.1 = s16[16,48,512]{2,1,0:T(8,128)(2,1)} async-done(((s16[16,48,512]{2,1,0:T(8,128)(2,1)}), s16[16,48,512]{2,1,0:T(8,128)(2,1)}, u32[]{:S(2)}, u32[]{:S(2)}) %all-to-all-start.1) | async-done | bytes 786464 | tf_op jit(solution)/shard_map/cond/branch_1_fun/all_to_all | solution.py:270
  87.5 26.3 %conditional.9 = (bf16[3750,128]{1,0:T(8,128)(2,1)}, s16[16,48,768]{2,1,0:T(8,128)(2,1)}, s16[16,48,512]{2,1,0:T(8,128)(2,1)}, f32[6,48,128]{2,1,0:T(8,128)S(1)}...) conditional(s32[]{:T(128)} %bitcast.32, () %tuple.58, ...), branch_computations={%region_6.7_spmd, %region_7.8_spmd} | conditional | flops 1480001 | bytes 17654762 | solution.py:259
  90.8 2.6 %collective-permute-start.21 = (bf16[3750,128]{1,0:T(8,128)(2,1)S(1)}, bf16[3750,128]{1,0:T(8,128)(2,1)}, u32[]{:S(2)}, u32[]{:S(2)}) collective-permute-start(bf16[3750,128]{1,0:T(8,128)(2,1)S(1)} %broadcast_select_fusion), channel_id=1, source_target_pairs={{0,32},{16,240},{32,64},{48,16},{64,96},{80,48},{96,128},{112,80},... | collective-permute-start | bytes 2880008 | tf_op jit(solution)/shard_map/cond/branch_1_fun/ppermute | solution.py:235
  93.4 5.5 %all-to-all-start.3 = ((s16[16,48,512]{2,1,0:T(8,128)(2,1)}), s16[16,48,512]{2,1,0:T(8,128)(2,1)}, u32[]{:S(2)}, u32[]{:S(2)}) async-start(s16[16,48,512]{2,1,0:T(8,128)(2,1)} %get-tuple-element.106), calls=%async_computation.3 | async-start | bytes 1572864 | tf_op jit(solution)/shard_map/cond/branch_1_fun/all_to_all | solution.py:270
  105.0 8.1 %project.8 = s16[16,48,768]{2,1,0:T(8,128)(2,1)} custom-call(bf16[768,3750]{1,0:T(8,128)(2,1)} %get-tuple-element.105.pd_ref, bf16[3750,128]{1,0:T(8,128)(2,1)} %get-tuple-element.103.refs_0_, bf16[3750,128]{1,0:T(8,128)(2,1)S(1)} %collective-permute-done.22.refs_1_, bf16[3750,128]{1,0:T(8,128)(2,1)} %get-tuple-element.104.refs_2_, ...), custom_call_target="tpu_custom_call" | custom-call | flops 1000000 | bytes 10000 | tf_op jit(solution)/shard_map/cond/branch_1_fun/project/pallas_call | solution.py:86
  113.8 33.8 %conditional.10 = (s16[16,48,768]{2,1,0:T(8,128)(2,1)}, f32[4,48,128]{2,1,0:T(8,128)S(1)}, bf16[4,48,128]{2,1,0:T(8,128)(2,1)S(1)}, bf16[2,128,2048]{2,1,0:T(8,1...) conditional(s32[]{:T(128)} %bitcast.32, () %tuple.65, (bf16[3750,128]{1,0:T(8,128)(2,1)}, ...), branch_computations={%region_8.9_spmd, %region_9.10_spmd} | conditional | flops 1000000 | bytes 19972480 | solution.py:259
  116.6 6.7 %project.9 = s16[16,48,768]{2,1,0:T(8,128)(2,1)} custom-call(bf16[768,3750]{1,0:T(8,128)(2,1)} %get-tuple-element.112.pd_ref, bf16[3750,128]{1,0:T(8,128)(2,1)} %get-tuple-element.113.refs_0_, bf16[3750,128]{1,0:T(8,128)(2,1)S(1)} %collective-permute-done.10.refs_1_, s16[16,48,768]{2,1,0:T(8,128)(2,1)} %get-tuple-element.114.refs_2_), custom_call_target="tpu_custom_call", output_to_operand_aliasing={{}: (3, {})} | custom-call | flops 1000000 | bytes 10000 | tf_op jit(solution)/shard_map/cond/branch_1_fun/project/pallas_call | solution.py:86
  123.3 5.3 %all-to-all-start.2 = ((s16[16,48,768]{2,1,0:T(8,128)(2,1)}), s16[16,48,768]{2,1,0:T(8,128)(2,1)}, u32[]{:S(2)}, u32[]{:S(2)}) async-start(s16[16,48,768]{2,1,0:T(8,128)(2,1)} %project.9), calls=%async_computation.2 | async-start | bytes 2359296 | tf_op jit(solution)/shard_map/cond/branch_1_fun/all_to_all | solution.py:270
  134.8 12.8 %all-to-all-done.2 = s16[16,48,768]{2,1,0:T(8,128)(2,1)} async-done(((s16[16,48,768]{2,1,0:T(8,128)(2,1)}), s16[16,48,768]{2,1,0:T(8,128)(2,1)}, u32[]{:S(2)}, u32[]{:S(2)}) %all-to-all-start.2) | async-done | bytes 1179680 | tf_op jit(solution)/shard_map/cond/branch_1_fun/all_to_all | solution.py:270
  147.6 9.9 %conditional.11 = (f32[10,48,128]{2,1,0:T(8,128)S(1)}, bf16[10,48,128]{2,1,0:T(8,128)(2,1)}, bf16[10,48,128]{2,1,0:T(8,128)(2,1)}, bf16[10,48,128]{2,1,0:T(8,128)(2,1)}, bf16[10,48,128]{2,1,0:T(8,128)(2,1)}) conditional(s32[]{:T(128)} %bitcast.32, () %tuple.64, (f32[48,1]{0,1:T(1,128)S(1)}, s16[16,48,768]{2,1,0:T(8,128)(2,1)}, ...), branch_computations={%region_10.11_spmd, %region_11.12_spmd} | conditional | bytes 1475104 | solution.py:259
  151.5 2.6 %collective-permute-done.16 = bf16[10,48,128]{2,1,0:T(8,128)(2,1)} collective-permute-done((bf16[10,48,128]{2,1,0:T(8,128)(2,1)}, bf16[10,48,128]{2,1,0:T(8,128)(2,1)}, u32[]{:S(2)}, u32[]{:S(2)}) %collective-permute-start.16) | collective-permute-done | bytes 122912 | tf_op jit(solution)/shard_map/cond/branch_1_fun/ppermute | solution.py:224
  157.7 6.4 %quad.1 = f32[16,56,128]{2,1,0:T(8,128)S(1)} custom-call(s32[16]{0:T(128)S(1)} %stack.106.refs_0_, s32[8]{0:T(128)S(1)} %stack.111.refs_1_, s32[8]{0:T(128)S(1)} %stack.114.refs_2_, f32[4,192]{1,0:T(4,128)S(1)} %get-tuple-element.167.refs_3_, f32[6,48,128]{2,1,0:T(8,128)S(1)} %get-tuple-element.182.refs_4_, f32[10,48,128]{2,1,0:T(8,128)S(1)} %get-tuple-element.191.refs_5_, ...), custom_call_target="tpu_custom_call" | custom-call | tf_op jit(solution)/shard_map/quad/pallas_call | solution.py:190
  164.1 16.7 %all_to_all.27 = f32[16,56,128]{2,1,0:T(8,128)S(1)} all-to-all(f32[16,56,128]{2,1,0:T(8,128)S(1)} %quad.1), channel_id=1, replica_groups=mesh['band'=16,'gvec'=16] {'gvec'}, dimensions={0} | all-to-all | bytes 917504 | tf_op jit(solution)/shard_map/all_to_all | solution.py:320
  181.5 6.0 %all-to-all-start.5 = ((f32[16,1,16]{2,1,0:T(1,128)}), f32[16,1,16]{2,1,0:T(1,128)S(1)}, u32[]{:S(2)}, u32[]{:S(2)}) async-start(f32[16,1,16]{2,1,0:T(1,128)} %broadcast_in_dim.30), calls=%async_computation.5 | async-start | bytes 16384 | tf_op jit(solution)/shard_map/all_to_all | solution.py:324
  188.3 6.2 %all-to-all-done.5 = f32[16,1,16]{2,1,0:T(1,128)S(1)} async-done(((f32[16,1,16]{2,1,0:T(1,128)}), f32[16,1,16]{2,1,0:T(1,128)S(1)}, u32[]{:S(2)}, u32[]{:S(2)}) %all-to-all-start.5) | async-done | bytes 1056 | tf_op jit(solution)/shard_map/all_to_all | solution.py:324
  (87 shorter events, 42.8 us)
Async XLA Ops:
  2.9 17.5 %collective-permute-start.19 = (bf16[3750,128]{1,0:T(8,128)(2,1)S(1)}, bf16[3750,128]{1,0:T(8,128)(2,1)S(1)}, u32[]{:S(2)}, u32[]{:S(2)}) collective-permute-start(bf16[3750,128]{1,0:T(8,128)(2,1)S(1)} %pad.3.refs_0_), channel_id=1, source_target_pairs={{0,16},{16,0},{32,48},{48,32},{64,80},{80,64},{96,112},{112,96},{1... | collective-permute-start | bytes 2880008 | tf_op jit(solution)/shard_map/cond/branch_1_fun/ppermute | solution.py:221
  6.2 24.5 %collective-permute-start.18 = (bf16[3750,128]{1,0:T(8,128)(2,1)S(1)}, bf16[3750,128]{1,0:T(8,128)(2,1)}, u32[]{:S(2)}, u32[]{:S(2)}) collective-permute-start(bf16[3750,128]{1,0:T(8,128)(2,1)S(1)} %pad.3.refs_0_), channel_id=1, source_target_pairs={{0,224},{16,240},{32,0},{48,16},{64,32},{80,48},{96,64},{112,80},{... | collective-permute-start | bytes 2880008 | tf_op jit(solution)/shard_map/cond/branch_1_fun/ppermute | solution.py:218
  10.1 23.8 %collective-permute-start.17 = (bf16[3750,128]{1,0:T(8,128)(2,1)S(1)}, bf16[3750,128]{1,0:T(8,128)(2,1)}, u32[]{:S(2)}, u32[]{:S(2)}) collective-permute-start(bf16[3750,128]{1,0:T(8,128)(2,1)S(1)} %pad.3.refs_0_), channel_id=1, source_target_pairs={{0,32},{16,48},{32,64},{48,80},{64,96},{80,112},{96,128},{112,144}... | collective-permute-start | bytes 2880008 | tf_op jit(solution)/shard_map/cond/branch_1_fun/ppermute | solution.py:218
  15.8 18.1 %collective-permute-start.20 = (bf16[2,128,2048]{2,1,0:T(8,128)(2,1)}, bf16[2,128,2048]{2,1,0:T(8,128)(2,1)}, u32[]{:S(2)}, u32[]{:S(2)}) collective-permute-start(bf16[2,128,2048]{2,1,0:T(8,128)(2,1)} %get-tuple-element.351), channel_id=1, source_target_pairs={{0,1},{1,2},{2,3},{3,0},{4,5},{5,6},{6,7},{7,4},{8,9},{9,10},{10,1... | collective-permute-start | bytes 3145736 | tf_op jit(solution)/shard_map/cond/branch_1_fun/ppermute | solution.py:232
  33.9 27.2 %collective-permute-start.4 = (bf16[2,128,2048]{2,1,0:T(8,128)(2,1)}, bf16[2,128,2048]{2,1,0:T(8,128)(2,1)}, u32[]{:S(2)}, u32[]{:S(2)}) collective-permute-start(bf16[2,128,2048]{2,1,0:T(8,128)(2,1)} %get-tuple-element.96), channel_id=1, source_target_pairs={{0,1},{1,2},{2,3},{3,0},{4,5},{5,6},{6,7},{7,4},{8,9},{9,10},{10,1... | collective-permute-start | bytes 3145736 | tf_op jit(solution)/shard_map/cond/branch_1_fun/ppermute | solution.py:232
  36.4 9.4 %collective-permute-start.2 = (bf16[3750,128]{1,0:T(8,128)(2,1)}, bf16[3750,128]{1,0:T(8,128)(2,1)S(1)}, u32[]{:S(2)}, u32[]{:S(2)}) collective-permute-start(bf16[3750,128]{1,0:T(8,128)(2,1)} %get-tuple-element.92.refs_0_), channel_id=1, source_target_pairs={{0,16},{16,0},{32,48},{48,32},{64,80},{80,64},{96,112},{112,96},{1... | collective-permute-start | bytes 2880008 | tf_op jit(solution)/shard_map/cond/branch_1_fun/ppermute | solution.py:221
  36.6 9.2 %collective-permute-start.3 = (bf16[3750,128]{1,0:T(8,128)(2,1)}, bf16[3750,128]{1,0:T(8,128)(2,1)S(1)}, u32[]{:S(2)}, u32[]{:S(2)}) collective-permute-start(bf16[3750,128]{1,0:T(8,128)(2,1)} %get-tuple-element.93.refs_2_), channel_id=1, source_target_pairs={{0,16},{16,0},{32,48},{48,32},{64,80},{80,64},{96,112},{112,96},{1... | collective-permute-start | bytes 2880008 | tf_op jit(solution)/shard_map/cond/branch_1_fun/ppermute | solution.py:221
  36.9 24.2 %collective-permute-start = (bf16[3750,128]{1,0:T(8,128)(2,1)}, bf16[3750,128]{1,0:T(8,128)(2,1)}, u32[]{:S(2)}, u32[]{:S(2)}) collective-permute-start(bf16[3750,128]{1,0:T(8,128)(2,1)} %get-tuple-element.92.refs_0_), channel_id=1, source_target_pairs={{0,32},{16,48},{32,64},{48,80},{64,96},{80,112},{96,128},{112,144}... | collective-permute-start | bytes 2880008 | tf_op jit(solution)/shard_map/cond/branch_1_fun/ppermute | solution.py:218
  36.9 24.2 %collective-permute-start.1 = (bf16[3750,128]{1,0:T(8,128)(2,1)}, bf16[3750,128]{1,0:T(8,128)(2,1)}, u32[]{:S(2)}, u32[]{:S(2)}) collective-permute-start(bf16[3750,128]{1,0:T(8,128)(2,1)} %get-tuple-element.93.refs_2_), channel_id=1, source_target_pairs={{0,224},{16,240},{32,0},{48,16},{64,32},{80,48},{96,64},{112,80},{... | collective-permute-start | bytes 2880008 | tf_op jit(solution)/shard_map/cond/branch_1_fun/ppermute | solution.py:218
  39.6 16.7 %all-to-all-start = ((s16[16,48,256]{2,1,0:T(8,128)(2,1)}), s16[16,48,256]{2,1,0:T(8,128)(2,1)}, u32[]{:S(2)}, u32[]{:S(2)}) async-start(s16[16,48,256]{2,1,0:T(8,128)(2,1)} %get-tuple-element.95), calls=%async_computation | async-start | bytes 786432 | tf_op jit(solution)/shard_map/cond/branch_1_fun/all_to_all | solution.py:270
  61.3 26.1 %collective-permute-start.9 = (bf16[2,128,2048]{2,1,0:T(8,128)(2,1)S(1)}, bf16[2,128,2048]{2,1,0:T(8,128)(2,1)}, u32[]{:S(2)}, u32[]{:S(2)}) collective-permute-start(bf16[2,128,2048]{2,1,0:T(8,128)(2,1)S(1)} %get-tuple-element.101), channel_id=1, source_target_pairs={{0,1},{1,2},{2,3},{3,0},{4,5},{5,6},{6,7},{7,4},{8,9},{9,10},{10,1... | collective-permute-start | bytes 3145736 | tf_op jit(solution)/shard_map/cond/branch_1_fun/ppermute | solution.py:232
  62.2 9.9 %collective-permute-start.7 = (bf16[3750,128]{1,0:T(8,128)(2,1)}, bf16[3750,128]{1,0:T(8,128)(2,1)S(1)}, u32[]{:S(2)}, u32[]{:S(2)}) collective-permute-start(bf16[3750,128]{1,0:T(8,128)(2,1)} %get-tuple-element.97.refs_0_), channel_id=1, source_target_pairs={{0,16},{16,0},{32,48},{48,32},{64,80},{80,64},{96,112},{112,96},{1... | collective-permute-start | bytes 2880008 | tf_op jit(solution)/shard_map/cond/branch_1_fun/ppermute | solution.py:221
  63.6 8.5 %collective-permute-start.8 = (bf16[3750,128]{1,0:T(8,128)(2,1)}, bf16[3750,128]{1,0:T(8,128)(2,1)S(1)}, u32[]{:S(2)}, u32[]{:S(2)}) collective-permute-start(bf16[3750,128]{1,0:T(8,128)(2,1)} %get-tuple-element.98.refs_2_), channel_id=1, source_target_pairs={{0,16},{16,0},{32,48},{48,32},{64,80},{80,64},{96,112},{112,96},{1... | collective-permute-start | bytes 2880008 | tf_op jit(solution)/shard_map/cond/branch_1_fun/ppermute | solution.py:221
  63.6 23.9 %collective-permute-start.5 = (bf16[3750,128]{1,0:T(8,128)(2,1)}, bf16[3750,128]{1,0:T(8,128)(2,1)}, u32[]{:S(2)}, u32[]{:S(2)}) collective-permute-start(bf16[3750,128]{1,0:T(8,128)(2,1)} %get-tuple-element.97.refs_0_), channel_id=1, source_target_pairs={{0,32},{16,48},{32,64},{48,80},{64,96},{80,112},{96,128},{112,144}... | collective-permute-start | bytes 2880008 | tf_op jit(solution)/shard_map/cond/branch_1_fun/ppermute | solution.py:218
  63.6 23.9 %collective-permute-start.6 = (bf16[3750,128]{1,0:T(8,128)(2,1)}, bf16[3750,128]{1,0:T(8,128)(2,1)}, u32[]{:S(2)}, u32[]{:S(2)}) collective-permute-start(bf16[3750,128]{1,0:T(8,128)(2,1)} %get-tuple-element.98.refs_2_), channel_id=1, source_target_pairs={{0,224},{16,240},{32,0},{48,16},{64,32},{80,48},{96,64},{112,80},{... | collective-permute-start | bytes 2880008 | tf_op jit(solution)/shard_map/cond/branch_1_fun/ppermute | solution.py:218
  66.3 20.8 %all-to-all-start.1 = ((s16[16,48,512]{2,1,0:T(8,128)(2,1)}), s16[16,48,512]{2,1,0:T(8,128)(2,1)}, u32[]{:S(2)}, u32[]{:S(2)}) async-start(s16[16,48,512]{2,1,0:T(8,128)(2,1)} %get-tuple-element.100), calls=%async_computation.1 | async-start | bytes 1572864 | tf_op jit(solution)/shard_map/cond/branch_1_fun/all_to_all | solution.py:270
  87.5 17.0 %collective-permute-start.23 = (bf16[3750,128]{1,0:T(8,128)(2,1)}, bf16[3750,128]{1,0:T(8,128)(2,1)S(1)}, u32[]{:S(2)}, u32[]{:S(2)}) collective-permute-start(bf16[3750,128]{1,0:T(8,128)(2,1)} %get-tuple-element.104.refs_2_), channel_id=1, source_target_pairs={{0,16},{16,0},{32,48},{48,32},{64,80},{80,64},{96,112},{112,96},{1... | collective-permute-start | bytes 2880008 | tf_op jit(solution)/shard_map/cond/branch_1_fun/ppermute | solution.py:221
  89.3 15.7 %collective-permute-start.22 = (bf16[3750,128]{1,0:T(8,128)(2,1)}, bf16[3750,128]{1,0:T(8,128)(2,1)S(1)}, u32[]{:S(2)}, u32[]{:S(2)}) collective-permute-start(bf16[3750,128]{1,0:T(8,128)(2,1)} %get-tuple-element.103.refs_0_), channel_id=1, source_target_pairs={{0,16},{16,0},{32,48},{48,32},{64,80},{80,64},{96,112},{112,96},{1... | collective-permute-start | bytes 2880008 | tf_op jit(solution)/shard_map/cond/branch_1_fun/ppermute | solution.py:221
  90.8 23.0 %collective-permute-start.21 = (bf16[3750,128]{1,0:T(8,128)(2,1)S(1)}, bf16[3750,128]{1,0:T(8,128)(2,1)}, u32[]{:S(2)}, u32[]{:S(2)}) collective-permute-start(bf16[3750,128]{1,0:T(8,128)(2,1)S(1)} %broadcast_select_fusion), channel_id=1, source_target_pairs={{0,32},{16,240},{32,64},{48,16},{64,96},{80,48},{96,128},{112,80},... | collective-permute-start | bytes 2880008 | tf_op jit(solution)/shard_map/cond/branch_1_fun/ppermute | solution.py:235
  93.4 20.4 %all-to-all-start.3 = ((s16[16,48,512]{2,1,0:T(8,128)(2,1)}), s16[16,48,512]{2,1,0:T(8,128)(2,1)}, u32[]{:S(2)}, u32[]{:S(2)}) async-start(s16[16,48,512]{2,1,0:T(8,128)(2,1)} %get-tuple-element.106), calls=%async_computation.3 | async-start | bytes 1572864 | tf_op jit(solution)/shard_map/cond/branch_1_fun/all_to_all | solution.py:270
  101.3 11.8 %collective-permute-start.26 = (bf16[6,48,128]{2,1,0:T(8,128)(2,1)}, bf16[6,48,128]{2,1,0:T(8,128)(2,1)}, u32[]{:S(2)}, u32[]{:S(2)}) collective-permute-start(bf16[6,48,128]{2,1,0:T(8,128)(2,1)} %get-tuple-element.388), channel_id=1, source_target_pairs={{0,12},{1,13},{2,14},{3,15},{4,0},{5,1},{6,2},{7,3},{8,4},{9,5},{1... | collective-permute-start | bytes 221192 | tf_op jit(solution)/shard_map/cond/branch_1_fun/ppermute | solution.py:224
  103.9 9.3 %collective-permute-start.25 = (bf16[6,48,128]{2,1,0:T(8,128)(2,1)}, bf16[6,48,128]{2,1,0:T(8,128)(2,1)}, u32[]{:S(2)}, u32[]{:S(2)}) collective-permute-start(bf16[6,48,128]{2,1,0:T(8,128)(2,1)} %get-tuple-element.388), channel_id=1, source_target_pairs={{0,8},{1,9},{2,10},{3,11},{4,12},{5,13},{6,14},{7,15},{8,0},{9,1},... | collective-permute-start | bytes 221192 | tf_op jit(solution)/shard_map/cond/branch_1_fun/ppermute | solution.py:224
  104.4 9.4 %collective-permute-start.24 = (bf16[6,48,128]{2,1,0:T(8,128)(2,1)}, bf16[6,48,128]{2,1,0:T(8,128)(2,1)}, u32[]{:S(2)}, u32[]{:S(2)}) collective-permute-start(bf16[6,48,128]{2,1,0:T(8,128)(2,1)} %get-tuple-element.388), channel_id=1, source_target_pairs={{0,4},{1,5},{2,6},{3,7},{4,8},{5,9},{6,10},{7,11},{8,12},{9,13},{1... | collective-permute-start | bytes 221192 | tf_op jit(solution)/shard_map/cond/branch_1_fun/ppermute | solution.py:224
  113.8 2.8 %collective-permute-start.10 = (bf16[3750,128]{1,0:T(8,128)(2,1)}, bf16[3750,128]{1,0:T(8,128)(2,1)S(1)}, u32[]{:S(2)}, u32[]{:S(2)}) collective-permute-start(bf16[3750,128]{1,0:T(8,128)(2,1)} %get-tuple-element.113.refs_0_), channel_id=1, source_target_pairs={{0,16},{16,0},{32,48},{48,32},{64,80},{80,64},{96,112},{112,96},{1... | collective-permute-start | bytes 2880008 | tf_op jit(solution)/shard_map/cond/branch_1_fun/ppermute | solution.py:221
  123.3 24.3 %all-to-all-start.2 = ((s16[16,48,768]{2,1,0:T(8,128)(2,1)}), s16[16,48,768]{2,1,0:T(8,128)(2,1)}, u32[]{:S(2)}, u32[]{:S(2)}) async-start(s16[16,48,768]{2,1,0:T(8,128)(2,1)} %project.9), calls=%async_computation.2 | async-start | bytes 2359296 | tf_op jit(solution)/shard_map/cond/branch_1_fun/all_to_all | solution.py:270
  128.6 3.1 %collective-permute-start.13 = (bf16[2,128,2048]{2,1,0:T(8,128)(2,1)}, bf16[2,128,2048]{2,1,0:T(8,128)(2,1)}, u32[]{:S(2)}, u32[]{:S(2)}) collective-permute-start(bf16[2,128,2048]{2,1,0:T(8,128)(2,1)} %get-tuple-element.121), channel_id=1, source_target_pairs={{0,16},{16,0},{32,48},{48,32},{64,80},{80,64},{96,112},{112,96},{1... | collective-permute-start | bytes 3145736 | tf_op jit(solution)/shard_map/cond/branch_1_fun/ppermute | solution.py:221
  129.2 4.1 %collective-permute-start.12 = (bf16[2,128,2048]{2,1,0:T(8,128)(2,1)}, bf16[2,128,2048]{2,1,0:T(8,128)(2,1)}, u32[]{:S(2)}, u32[]{:S(2)}) collective-permute-start(bf16[2,128,2048]{2,1,0:T(8,128)(2,1)} %get-tuple-element.120), channel_id=1, source_target_pairs={{0,16},{16,0},{32,48},{48,32},{64,80},{80,64},{96,112},{112,96},{1... | collective-permute-start | bytes 3145736 | tf_op jit(solution)/shard_map/cond/branch_1_fun/ppermute | solution.py:221
  129.3 5.5 %collective-permute-start.11 = (bf16[2,128,2048]{2,1,0:T(8,128)(2,1)}, bf16[2,128,2048]{2,1,0:T(8,128)(2,1)}, u32[]{:S(2)}, u32[]{:S(2)}) collective-permute-start(bf16[2,128,2048]{2,1,0:T(8,128)(2,1)} %get-tuple-element.119), channel_id=1, source_target_pairs={{0,16},{16,0},{32,48},{48,32},{64,80},{80,64},{96,112},{112,96},{1... | collective-permute-start | bytes 3145736 | tf_op jit(solution)/shard_map/cond/branch_1_fun/ppermute | solution.py:221
  150.1 4.0 %collective-permute-start.16 = (bf16[10,48,128]{2,1,0:T(8,128)(2,1)}, bf16[10,48,128]{2,1,0:T(8,128)(2,1)}, u32[]{:S(2)}, u32[]{:S(2)}) collective-permute-start(bf16[10,48,128]{2,1,0:T(8,128)(2,1)} %get-tuple-element.410), channel_id=1, source_target_pairs={{0,12},{1,13},{2,14},{3,15},{4,0},{5,1},{6,2},{7,3},{8,4},{9,5},{1... | collective-permute-start | bytes 368648 | tf_op jit(solution)/shard_map/cond/branch_1_fun/ppermute | solution.py:224
  150.4 5.6 %collective-permute-start.15 = (bf16[10,48,128]{2,1,0:T(8,128)(2,1)}, bf16[10,48,128]{2,1,0:T(8,128)(2,1)}, u32[]{:S(2)}, u32[]{:S(2)}) collective-permute-start(bf16[10,48,128]{2,1,0:T(8,128)(2,1)} %get-tuple-element.410), channel_id=1, source_target_pairs={{0,8},{1,9},{2,10},{3,11},{4,12},{5,13},{6,14},{7,15},{8,0},{9,1},... | collective-permute-start | bytes 368648 | tf_op jit(solution)/shard_map/cond/branch_1_fun/ppermute | solution.py:224
  151.4 6.1 %collective-permute-start.14 = (bf16[10,48,128]{2,1,0:T(8,128)(2,1)}, bf16[10,48,128]{2,1,0:T(8,128)(2,1)}, u32[]{:S(2)}, u32[]{:S(2)}) collective-permute-start(bf16[10,48,128]{2,1,0:T(8,128)(2,1)} %get-tuple-element.410), channel_id=1, source_target_pairs={{0,4},{1,5},{2,6},{3,7},{4,8},{5,9},{6,10},{7,11},{8,12},{9,13},{1... | collective-permute-start | bytes 368648 | tf_op jit(solution)/shard_map/cond/branch_1_fun/ppermute | solution.py:224
  181.5 13.0 %all-to-all-start.5 = ((f32[16,1,16]{2,1,0:T(1,128)}), f32[16,1,16]{2,1,0:T(1,128)S(1)}, u32[]{:S(2)}, u32[]{:S(2)}) async-start(f32[16,1,16]{2,1,0:T(1,128)} %broadcast_in_dim.30), calls=%async_computation.5 | async-start | bytes 16384 | tf_op jit(solution)/shard_map/all_to_all | solution.py:324
  (3 other events, 39.8 us)

commit v2 on v1

--- a/solution.py
+++ b/solution.py
@@ -14,6 +14,7 @@
 SIDE = 4
 GROUPS = ((0, 2), (2, 5))
 SPLIT = 4
+JOIN = 2
 MEGA = 1024 * 1024
 ANYWHERE = pl.BlockSpec(memory_space=pl.ANY)
 IN_VMEM = pl.BlockSpec(memory_space=pltpu.VMEM)
@@ -160,22 +161,28 @@
     right = flat[...]
     count = weights[0].shape[0]
 
-    def add(i, total):
-        pltpu.make_async_copy(store.at[0:count], store.at[pl.ds(i * count, count)], sems.at[i]).wait()
-        lane = pl.ds(pl.multiple_of(own_ref[i] * LANES, LANES), LANES)
-        left = flat[:, lane].astype(jnp.float32).T
+    def add(step, total):
+        span = pl.ds(step * JOIN * count, JOIN * count)
+        for j in range(JOIN):
+            i = step * JOIN + j
+            pltpu.make_async_copy(store.at[0:count], store.at[pl.ds(i * count, count)], sems.at[i]).wait()
         applied = lax.dot_general(
-            store[pl.ds(i * count, count)].reshape(count * LANES, store.shape[2]),
+            store[span].reshape(JOIN * count * LANES, store.shape[2]),
             right,
             (((1,), (1,)), ((), ())),
             preferred_element_type=jnp.float32,
         )
-        for n in range(count):
-            value = jnp.sum(left * applied[n * LANES : (n + 1) * LANES], axis=0, keepdims=True)
-            total += value * pick_ref[pl.ds(node_ref[i] + n, 1), :]
+        for j in range(JOIN):
+            i = step * JOIN + j
+            lane = pl.ds(pl.multiple_of(own_ref[i] * LANES, LANES), LANES)
+            left = flat[:, lane].astype(jnp.float32).T
+            for n in range(count):
+                part = applied[(j * count + n) * LANES : (j * count + n + 1) * LANES]
+                value = jnp.sum(left * part, axis=0, keepdims=True)
+                total += value * pick_ref[pl.ds(node_ref[i] + n, 1), :]
         return total
 
-    total = lax.fori_loop(0, tables, add, jnp.zeros((1, SIDE * rows), jnp.float32))
+    total = lax.fori_loop(0, tables // JOIN, add, jnp.zeros((1, SIDE * rows), jnp.float32))
     first = jnp.zeros((8, LANES), jnp.float32)
     line = lax.broadcasted_iota(jnp.int32, (8, LANES), 0)
     rest = jnp.concatenate([total[:, LANES:], jnp.zeros((1, 2 * LANES - SIDE * rows), jnp.float32)], axis=1)

time: 196 us -> 196 us (level)
  no operation moved by 1% of the time
where the time goes in v2:
time: 196 us; the launch traced here: 195 us
  starting transfers between devices  60.3 us (31%)
  waiting for transfers between devices  53.4 us (27%)
  Pallas kernels  52.2 us (27%)
  blocking collectives  16.7 us (9%)
  local copies, waits for them, and re-layouts  6.69 us (3%)
  other arithmetic  3.58 us (2%)
    pallas_call x5, Pallas kernels, project(): pl.pallas_call(lambda pd_ref, *refs: project_kernel(shape, pd_ref, *refs[...  37.4 us
    all_to_all x4, starting transfers between devices, send(): return lax.all_to_all(code, 'gvec', 0, 0)  22.8 us
    all_to_all x4, waiting for transfers between devices, send(): return lax.all_to_all(code, 'gvec', 0, 0)  22 us
    all_to_all x1, blocking collectives, local(): landed = lax.all_to_all(message, 'gvec', 0, 0)  16.7 us
    ppermute x6, waiting for transfers between devices, shift(): lax.ppermute(value, 'band', [(b, (b + 2 * by) % bands) for b in range(ban...  12.4 us
    ppermute x6, starting transfers between devices, shift(): lax.ppermute(value, 'band', [(b, (b + 2 * by) % bands) for b in range(ban...  9.21 us
    ppermute x11, starting transfers between devices, sibling(): return lax.ppermute(value, 'band', [(b, b ^ 1) for b in range(bands)])  8.67 us
    ppermute x6, waiting for transfers between devices, along_y(): lax.ppermute(value, 'gvec', [(g, (g + SIDE * by) % devices) for g in rang...  6.68 us
  transfers between devices with their start and end apart: 32, of which 16 were waited for; matrix products, arithmetic and copies ran while one was open for 4% of the time, Pallas kernels for 19%

profile of v2, /device:TPU:1, one launch (start us, length us, event | category | flops | bytes accessed | tf_op | source)
XLA Modules:
  0.0 194.6 jit_solution(16197073175738403071)
XLA Ops:
  1.5 32.4 %conditional.6 = (bf16[3750,128]{1,0:T(8,128)(2,1)}, bf16[3750,128]{1,0:T(8,128)(2,1)}, s16[16,48,256]{2,1,0:T(8,128)(2,1)}, bf16[2,128,2048]{2,1,0:T(8,128)(2,1...) conditional(s32[]{:T(128)} %bitcast.32, () %tuple.56, ...), branch_computations={%region_0.0_spmd, %region_1.2_spmd} | conditional | flops 1003006 | bytes 21678728 | solution.py:266
  2.9 3.3 %collective-permute-start.19 = (bf16[3750,128]{1,0:T(8,128)(2,1)S(1)}, bf16[3750,128]{1,0:T(8,128)(2,1)S(1)}, u32[]{:S(2)}, u32[]{:S(2)}) collective-permute-start(bf16[3750,128]{1,0:T(8,128)(2,1)S(1)} %pad.3.refs_0_), channel_id=1, source_target_pairs={{0,16},{16,0},{32,48},{48,32},{64,80},{80,64},{96,112},{112,96},{1... | collective-permute-start | bytes 2880008 | tf_op jit(solution)/shard_map/cond/branch_1_fun/ppermute | solution.py:228
  6.2 3.9 %collective-permute-start.18 = (bf16[3750,128]{1,0:T(8,128)(2,1)S(1)}, bf16[3750,128]{1,0:T(8,128)(2,1)}, u32[]{:S(2)}, u32[]{:S(2)}) collective-permute-start(bf16[3750,128]{1,0:T(8,128)(2,1)S(1)} %pad.3.refs_0_), channel_id=1, source_target_pairs={{0,224},{16,240},{32,0},{48,16},{64,32},{80,48},{96,64},{112,80},{... | collective-permute-start | bytes 2880008 | tf_op jit(solution)/shard_map/cond/branch_1_fun/ppermute | solution.py:225
  10.1 2.7 %copy.28.w_ref = bf16[4,125,2000]{2,1,0:T(8,128)(2,1)S(1)} copy(bf16[4,125,2000]{2,0,1:T(4,128)(2,1)} %get-tuple-element.305) | data formatting | bytes 4000000 | tf_op jit(solution)/shard_map
  12.8 2.9 %spread.1 = (bf16[2,128,2048]{2,1,0:T(8,128)(2,1)}, bf16[2,128,2048]{2,1,0:T(8,128)(2,1)S(1)}) custom-call(s32[2]{0:T(128)S(1)} %get-tuple-element.82.first_ref, bf16[4,125,2000]{2,1,0:T(8,128)(2,1)S(1)} %copy.28.w_ref), custom_call_target="tpu_custom_call" | custom-call | tf_op jit(solution)/shard_map/cond/branch_1_fun/spread/pallas_call | solution.py:47
  20.4 6.4 %project.5 = s16[16,48,256]{2,1,0:T(8,128)(2,1)} custom-call(bf16[768,3750]{1,0:T(8,128)(2,1)} %get-tuple-element.81.pd_ref, bf16[3750,128]{1,0:T(8,128)(2,1)S(1)} %pad.3.refs_0_, bf16[3750,128]{1,0:T(8,128)(2,1)S(1)} %collective-permute-done.19.refs_1_), custom_call_target="tpu_custom_call" | custom-call | flops 1000000 | bytes 10000 | tf_op jit(solution)/shard_map/cond/branch_1_fun/project/pallas_call | solution.py:87
  26.7 4.0 %collective-permute-done.18 = bf16[3750,128]{1,0:T(8,128)(2,1)} collective-permute-done((bf16[3750,128]{1,0:T(8,128)(2,1)S(1)}, bf16[3750,128]{1,0:T(8,128)(2,1)}, u32[]{:S(2)}, u32[]{:S(2)}) %collective-permute-start.18) | collective-permute-done | bytes 960032 | tf_op jit(solution)/shard_map/cond/branch_1_fun/ppermute | solution.py:225
  30.7 3.2 %collective-permute-done.17 = bf16[3750,128]{1,0:T(8,128)(2,1)} collective-permute-done((bf16[3750,128]{1,0:T(8,128)(2,1)S(1)}, bf16[3750,128]{1,0:T(8,128)(2,1)}, u32[]{:S(2)}, u32[]{:S(2)}) %collective-permute-start.17) | collective-permute-done | bytes 960032 | tf_op jit(solution)/shard_map/cond/branch_1_fun/ppermute | solution.py:225
  33.9 27.2 %conditional.7 = (bf16[3750,128]{1,0:T(8,128)(2,1)}, bf16[3750,128]{1,0:T(8,128)(2,1)}, s16[16,48,512]{2,1,0:T(8,128)(2,1)}, s16[16,48,256]{2,1,0:T(8,128)(2,1)}, bf16[2,128,2048]{2,1,0:T(8,128)(2,1)}) conditional(s32[]{:T(128)} %bitcast.32, () %tuple.60, (bf16[3750,128]{1,0:T(8,128)(2,1)}, bf16[3750,128]{1,0:T(8,128)(2,1)}, ...), branch_computations={%region_2.3_spmd, %region_3.4_spmd} | conditional | flops 1000000 | bytes 20744224 | solution.py:266
  36.9 2.7 %collective-permute-start.1 = (bf16[3750,128]{1,0:T(8,128)(2,1)}, bf16[3750,128]{1,0:T(8,128)(2,1)}, u32[]{:S(2)}, u32[]{:S(2)}) collective-permute-start(bf16[3750,128]{1,0:T(8,128)(2,1)} %get-tuple-element.93.refs_2_), channel_id=1, source_target_pairs={{0,224},{16,240},{32,0},{48,16},{64,32},{80,48},{96,64},{112,80},{... | collective-permute-start | bytes 2880008 | tf_op jit(solution)/shard_map/cond/branch_1_fun/ppermute | solution.py:225
  39.6 6.2 %all-to-all-start = ((s16[16,48,256]{2,1,0:T(8,128)(2,1)}), s16[16,48,256]{2,1,0:T(8,128)(2,1)}, u32[]{:S(2)}, u32[]{:S(2)}) async-start(s16[16,48,256]{2,1,0:T(8,128)(2,1)} %get-tuple-element.95), calls=%async_computation | async-start | bytes 786432 | tf_op jit(solution)/shard_map/cond/branch_1_fun/all_to_all | solution.py:277
  45.8 8.1 %project.6 = s16[16,48,512]{2,1,0:T(8,128)(2,1)} custom-call(bf16[768,3750]{1,0:T(8,128)(2,1)} %get-tuple-element.94.pd_ref, bf16[3750,128]{1,0:T(8,128)(2,1)} %get-tuple-element.92.refs_0_, bf16[3750,128]{1,0:T(8,128)(2,1)S(1)} %collective-permute-done.2.refs_1_, bf16[3750,128]{1,0:T(8,128)(2,1)} %get-tuple-element.93.refs_2_, ...), custom_call_target="tpu_custom_call" | custom-call | flops 1000000 | bytes 10000 | tf_op jit(solution)/shard_map/cond/branch_1_fun/project/pallas_call | solution.py:87
  56.3 4.9 %collective-permute-done = bf16[3750,128]{1,0:T(8,128)(2,1)} collective-permute-done((bf16[3750,128]{1,0:T(8,128)(2,1)}, bf16[3750,128]{1,0:T(8,128)(2,1)}, u32[]{:S(2)}, u32[]{:S(2)}) %collective-permute-start) | collective-permute-done | bytes 960032 | tf_op jit(solution)/shard_map/cond/branch_1_fun/ppermute | solution.py:225
  61.1 26.3 %conditional.8 = (bf16[3750,128]{1,0:T(8,128)(2,1)}, bf16[3750,128]{1,0:T(8,128)(2,1)}, s16[16,48,512]{2,1,0:T(8,128)(2,1)}, s16[16,48,512]{2,1,0:T(8,128)(2,1)}, bf16[2,128,2048]{2,1,0:T(8,128)(2,1)}) conditional(s32[]{:T(128)} %bitcast.32, () %tuple.59, (bf16[3750,128]{1,0:T(8,128)(2,1)}, bf16[3750,128]{1,0:T(8,128)(2,1)}, ...), branch_computations={%region_4.5_spmd, %region_5.6_spmd} | conditional | flops 1000000 | bytes 21923872 | solution.py:266
  63.6 2.7 %collective-permute-start.6 = (bf16[3750,128]{1,0:T(8,128)(2,1)}, bf16[3750,128]{1,0:T(8,128)(2,1)}, u32[]{:S(2)}, u32[]{:S(2)}) collective-permute-start(bf16[3750,128]{1,0:T(8,128)(2,1)} %get-tuple-element.98.refs_2_), channel_id=1, source_target_pairs={{0,224},{16,240},{32,0},{48,16},{64,32},{80,48},{96,64},{112,80},{... | collective-permute-start | bytes 2880008 | tf_op jit(solution)/shard_map/cond/branch_1_fun/ppermute | solution.py:225
  66.3 5.8 %all-to-all-start.1 = ((s16[16,48,512]{2,1,0:T(8,128)(2,1)}), s16[16,48,512]{2,1,0:T(8,128)(2,1)}, u32[]{:S(2)}, u32[]{:S(2)}) async-start(s16[16,48,512]{2,1,0:T(8,128)(2,1)} %get-tuple-element.100), calls=%async_computation.1 | async-start | bytes 1572864 | tf_op jit(solution)/shard_map/cond/branch_1_fun/all_to_all | solution.py:277
  72.1 8.1 %project.7 = s16[16,48,512]{2,1,0:T(8,128)(2,1)} custom-call(bf16[768,3750]{1,0:T(8,128)(2,1)} %get-tuple-element.99.pd_ref, bf16[3750,128]{1,0:T(8,128)(2,1)} %get-tuple-element.97.refs_0_, bf16[3750,128]{1,0:T(8,128)(2,1)S(1)} %collective-permute-done.7.refs_1_, bf16[3750,128]{1,0:T(8,128)(2,1)} %get-tuple-element.98.refs_2_, ...), custom_call_target="tpu_custom_call" | custom-call | flops 1000000 | bytes 10000 | tf_op jit(solution)/shard_map/cond/branch_1_fun/project/pallas_call | solution.py:87
  80.3 6.8 %all-to-all-done.1 = s16[16,48,512]{2,1,0:T(8,128)(2,1)} async-done(((s16[16,48,512]{2,1,0:T(8,128)(2,1)}), s16[16,48,512]{2,1,0:T(8,128)(2,1)}, u32[]{:S(2)}, u32[]{:S(2)}) %all-to-all-start.1) | async-done | bytes 786464 | tf_op jit(solution)/shard_map/cond/branch_1_fun/all_to_all | solution.py:277
  87.5 26.3 %conditional.9 = (bf16[3750,128]{1,0:T(8,128)(2,1)}, s16[16,48,768]{2,1,0:T(8,128)(2,1)}, s16[16,48,512]{2,1,0:T(8,128)(2,1)}, f32[6,48,128]{2,1,0:T(8,128)S(1)}...) conditional(s32[]{:T(128)} %bitcast.32, () %tuple.58, ...), branch_computations={%region_6.7_spmd, %region_7.8_spmd} | conditional | flops 1480001 | bytes 17654762 | solution.py:266
  90.8 2.6 %collective-permute-start.21 = (bf16[3750,128]{1,0:T(8,128)(2,1)S(1)}, bf16[3750,128]{1,0:T(8,128)(2,1)}, u32[]{:S(2)}, u32[]{:S(2)}) collective-permute-start(bf16[3750,128]{1,0:T(8,128)(2,1)S(1)} %broadcast_select_fusion), channel_id=1, source_target_pairs={{0,32},{16,240},{32,64},{48,16},{64,96},{80,48},{96,128},{112,80},... | collective-permute-start | bytes 2880008 | tf_op jit(solution)/shard_map/cond/branch_1_fun/ppermute | solution.py:242
  93.4 5.5 %all-to-all-start.3 = ((s16[16,48,512]{2,1,0:T(8,128)(2,1)}), s16[16,48,512]{2,1,0:T(8,128)(2,1)}, u32[]{:S(2)}, u32[]{:S(2)}) async-start(s16[16,48,512]{2,1,0:T(8,128)(2,1)} %get-tuple-element.106), calls=%async_computation.3 | async-start | bytes 1572864 | tf_op jit(solution)/shard_map/cond/branch_1_fun/all_to_all | solution.py:277
  105.0 8.1 %project.8 = s16[16,48,768]{2,1,0:T(8,128)(2,1)} custom-call(bf16[768,3750]{1,0:T(8,128)(2,1)} %get-tuple-element.105.pd_ref, bf16[3750,128]{1,0:T(8,128)(2,1)} %get-tuple-element.103.refs_0_, bf16[3750,128]{1,0:T(8,128)(2,1)S(1)} %collective-permute-done.22.refs_1_, bf16[3750,128]{1,0:T(8,128)(2,1)} %get-tuple-element.104.refs_2_, ...), custom_call_target="tpu_custom_call" | custom-call | flops 1000000 | bytes 10000 | tf_op jit(solution)/shard_map/cond/branch_1_fun/project/pallas_call | solution.py:87
  113.8 33.8 %conditional.10 = (s16[16,48,768]{2,1,0:T(8,128)(2,1)}, f32[4,48,128]{2,1,0:T(8,128)S(1)}, bf16[4,48,128]{2,1,0:T(8,128)(2,1)S(1)}, bf16[2,128,2048]{2,1,0:T(8,1...) conditional(s32[]{:T(128)} %bitcast.32, () %tuple.65, (bf16[3750,128]{1,0:T(8,128)(2,1)}, ...), branch_computations={%region_8.9_spmd, %region_9.10_spmd} | conditional | flops 1000000 | bytes 19972480 | solution.py:266
  116.6 6.7 %project.9 = s16[16,48,768]{2,1,0:T(8,128)(2,1)} custom-call(bf16[768,3750]{1,0:T(8,128)(2,1)} %get-tuple-element.112.pd_ref, bf16[3750,128]{1,0:T(8,128)(2,1)} %get-tuple-element.113.refs_0_, bf16[3750,128]{1,0:T(8,128)(2,1)S(1)} %collective-permute-done.10.refs_1_, s16[16,48,768]{2,1,0:T(8,128)(2,1)} %get-tuple-element.114.refs_2_), custom_call_target="tpu_custom_call", output_to_operand_aliasing={{}: (3, {})} | custom-call | flops 1000000 | bytes 10000 | tf_op jit(solution)/shard_map/cond/branch_1_fun/project/pallas_call | solution.py:87
  123.3 5.3 %all-to-all-start.2 = ((s16[16,48,768]{2,1,0:T(8,128)(2,1)}), s16[16,48,768]{2,1,0:T(8,128)(2,1)}, u32[]{:S(2)}, u32[]{:S(2)}) async-start(s16[16,48,768]{2,1,0:T(8,128)(2,1)} %project.9), calls=%async_computation.2 | async-start | bytes 2359296 | tf_op jit(solution)/shard_map/cond/branch_1_fun/all_to_all | solution.py:277
  134.8 12.8 %all-to-all-done.2 = s16[16,48,768]{2,1,0:T(8,128)(2,1)} async-done(((s16[16,48,768]{2,1,0:T(8,128)(2,1)}), s16[16,48,768]{2,1,0:T(8,128)(2,1)}, u32[]{:S(2)}, u32[]{:S(2)}) %all-to-all-start.2) | async-done | bytes 1179680 | tf_op jit(solution)/shard_map/cond/branch_1_fun/all_to_all | solution.py:277
  147.6 9.9 %conditional.11 = (f32[10,48,128]{2,1,0:T(8,128)S(1)}, bf16[10,48,128]{2,1,0:T(8,128)(2,1)}, bf16[10,48,128]{2,1,0:T(8,128)(2,1)}, bf16[10,48,128]{2,1,0:T(8,128)(2,1)}, bf16[10,48,128]{2,1,0:T(8,128)(2,1)}) conditional(s32[]{:T(128)} %bitcast.32, () %tuple.64, (f32[48,1]{0,1:T(1,128)S(1)}, s16[16,48,768]{2,1,0:T(8,128)(2,1)}, ...), branch_computations={%region_10.11_spmd, %region_11.12_spmd} | conditional | bytes 1475104 | solution.py:266
  151.5 2.6 %collective-permute-done.16 = bf16[10,48,128]{2,1,0:T(8,128)(2,1)} collective-permute-done((bf16[10,48,128]{2,1,0:T(8,128)(2,1)}, bf16[10,48,128]{2,1,0:T(8,128)(2,1)}, u32[]{:S(2)}, u32[]{:S(2)}) %collective-permute-start.16) | collective-permute-done | bytes 122912 | tf_op jit(solution)/shard_map/cond/branch_1_fun/ppermute | solution.py:231
  157.7 5.8 %quad.1 = f32[16,56,128]{2,1,0:T(8,128)S(1)} custom-call(s32[16]{0:T(128)S(1)} %stack.106.refs_0_, s32[8]{0:T(128)S(1)} %stack.111.refs_1_, s32[8]{0:T(128)S(1)} %stack.114.refs_2_, f32[4,192]{1,0:T(4,128)S(1)} %get-tuple-element.167.refs_3_, f32[6,48,128]{2,1,0:T(8,128)S(1)} %get-tuple-element.182.refs_4_, f32[10,48,128]{2,1,0:T(8,128)S(1)} %get-tuple-element.191.refs_5_, ...), custom_call_target="tpu_custom_call" | custom-call | tf_op jit(solution)/shard_map/quad/pallas_call | solution.py:197
  163.6 16.7 %all_to_all.27 = f32[16,56,128]{2,1,0:T(8,128)S(1)} all-to-all(f32[16,56,128]{2,1,0:T(8,128)S(1)} %quad.1), channel_id=1, replica_groups=mesh['band'=16,'gvec'=16] {'gvec'}, dimensions={0} | all-to-all | bytes 917504 | tf_op jit(solution)/shard_map/all_to_all | solution.py:327
  181.0 6.0 %all-to-all-start.5 = ((f32[16,1,16]{2,1,0:T(1,128)}), f32[16,1,16]{2,1,0:T(1,128)S(1)}, u32[]{:S(2)}, u32[]{:S(2)}) async-start(f32[16,1,16]{2,1,0:T(1,128)} %broadcast_in_dim.30), calls=%async_computation.5 | async-start | bytes 16384 | tf_op jit(solution)/shard_map/all_to_all | solution.py:331
  187.8 6.2 %all-to-all-done.5 = f32[16,1,16]{2,1,0:T(1,128)S(1)} async-done(((f32[16,1,16]{2,1,0:T(1,128)}), f32[16,1,16]{2,1,0:T(1,128)S(1)}, u32[]{:S(2)}, u32[]{:S(2)}) %all-to-all-start.5) | async-done | bytes 1056 | tf_op jit(solution)/shard_map/all_to_all | solution.py:331
  (87 shorter events, 42.8 us)
Async XLA Ops:
  2.9 17.5 %collective-permute-start.19 = (bf16[3750,128]{1,0:T(8,128)(2,1)S(1)}, bf16[3750,128]{1,0:T(8,128)(2,1)S(1)}, u32[]{:S(2)}, u32[]{:S(2)}) collective-permute-start(bf16[3750,128]{1,0:T(8,128)(2,1)S(1)} %pad.3.refs_0_), channel_id=1, source_target_pairs={{0,16},{16,0},{32,48},{48,32},{64,80},{80,64},{96,112},{112,96},{1... | collective-permute-start | bytes 2880008 | tf_op jit(solution)/shard_map/cond/branch_1_fun/ppermute | solution.py:228
  6.2 24.5 %collective-permute-start.18 = (bf16[3750,128]{1,0:T(8,128)(2,1)S(1)}, bf16[3750,128]{1,0:T(8,128)(2,1)}, u32[]{:S(2)}, u32[]{:S(2)}) collective-permute-start(bf16[3750,128]{1,0:T(8,128)(2,1)S(1)} %pad.3.refs_0_), channel_id=1, source_target_pairs={{0,224},{16,240},{32,0},{48,16},{64,32},{80,48},{96,64},{112,80},{... | collective-permute-start | bytes 2880008 | tf_op jit(solution)/shard_map/cond/branch_1_fun/ppermute | solution.py:225
  10.1 23.8 %collective-permute-start.17 = (bf16[3750,128]{1,0:T(8,128)(2,1)S(1)}, bf16[3750,128]{1,0:T(8,128)(2,1)}, u32[]{:S(2)}, u32[]{:S(2)}) collective-permute-start(bf16[3750,128]{1,0:T(8,128)(2,1)S(1)} %pad.3.refs_0_), channel_id=1, source_target_pairs={{0,32},{16,48},{32,64},{48,80},{64,96},{80,112},{96,128},{112,144}... | collective-permute-start | bytes 2880008 | tf_op jit(solution)/shard_map/cond/branch_1_fun/ppermute | solution.py:225
  15.8 18.1 %collective-permute-start.20 = (bf16[2,128,2048]{2,1,0:T(8,128)(2,1)}, bf16[2,128,2048]{2,1,0:T(8,128)(2,1)}, u32[]{:S(2)}, u32[]{:S(2)}) collective-permute-start(bf16[2,128,2048]{2,1,0:T(8,128)(2,1)} %get-tuple-element.351), channel_id=1, source_target_pairs={{0,1},{1,2},{2,3},{3,0},{4,5},{5,6},{6,7},{7,4},{8,9},{9,10},{10,1... | collective-permute-start | bytes 3145736 | tf_op jit(solution)/shard_map/cond/branch_1_fun/ppermute | solution.py:239
  33.9 27.2 %collective-permute-start.4 = (bf16[2,128,2048]{2,1,0:T(8,128)(2,1)}, bf16[2,128,2048]{2,1,0:T(8,128)(2,1)}, u32[]{:S(2)}, u32[]{:S(2)}) collective-permute-start(bf16[2,128,2048]{2,1,0:T(8,128)(2,1)} %get-tuple-element.96), channel_id=1, source_target_pairs={{0,1},{1,2},{2,3},{3,0},{4,5},{5,6},{6,7},{7,4},{8,9},{9,10},{10,1... | collective-permute-start | bytes 3145736 | tf_op jit(solution)/shard_map/cond/branch_1_fun/ppermute | solution.py:239
  36.4 9.4 %collective-permute-start.2 = (bf16[3750,128]{1,0:T(8,128)(2,1)}, bf16[3750,128]{1,0:T(8,128)(2,1)S(1)}, u32[]{:S(2)}, u32[]{:S(2)}) collective-permute-start(bf16[3750,128]{1,0:T(8,128)(2,1)} %get-tuple-element.92.refs_0_), channel_id=1, source_target_pairs={{0,16},{16,0},{32,48},{48,32},{64,80},{80,64},{96,112},{112,96},{1... | collective-permute-start | bytes 2880008 | tf_op jit(solution)/shard_map/cond/branch_1_fun/ppermute | solution.py:228
  36.6 9.2 %collective-permute-start.3 = (bf16[3750,128]{1,0:T(8,128)(2,1)}, bf16[3750,128]{1,0:T(8,128)(2,1)S(1)}, u32[]{:S(2)}, u32[]{:S(2)}) collective-permute-start(bf16[3750,128]{1,0:T(8,128)(2,1)} %get-tuple-element.93.refs_2_), channel_id=1, source_target_pairs={{0,16},{16,0},{32,48},{48,32},{64,80},{80,64},{96,112},{112,96},{1... | collective-permute-start | bytes 2880008 | tf_op jit(solution)/shard_map/cond/branch_1_fun/ppermute | solution.py:228
  36.9 24.2 %collective-permute-start = (bf16[3750,128]{1,0:T(8,128)(2,1)}, bf16[3750,128]{1,0:T(8,128)(2,1)}, u32[]{:S(2)}, u32[]{:S(2)}) collective-permute-start(bf16[3750,128]{1,0:T(8,128)(2,1)} %get-tuple-element.92.refs_0_), channel_id=1, source_target_pairs={{0,32},{16,48},{32,64},{48,80},{64,96},{80,112},{96,128},{112,144}... | collective-permute-start | bytes 2880008 | tf_op jit(solution)/shard_map/cond/branch_1_fun/ppermute | solution.py:225
  36.9 24.2 %collective-permute-start.1 = (bf16[3750,128]{1,0:T(8,128)(2,1)}, bf16[3750,128]{1,0:T(8,128)(2,1)}, u32[]{:S(2)}, u32[]{:S(2)}) collective-permute-start(bf16[3750,128]{1,0:T(8,128)(2,1)} %get-tuple-element.93.refs_2_), channel_id=1, source_target_pairs={{0,224},{16,240},{32,0},{48,16},{64,32},{80,48},{96,64},{112,80},{... | collective-permute-start | bytes 2880008 | tf_op jit(solution)/shard_map/cond/branch_1_fun/ppermute | solution.py:225
  39.6 16.7 %all-to-all-start = ((s16[16,48,256]{2,1,0:T(8,128)(2,1)}), s16[16,48,256]{2,1,0:T(8,128)(2,1)}, u32[]{:S(2)}, u32[]{:S(2)}) async-start(s16[16,48,256]{2,1,0:T(8,128)(2,1)} %get-tuple-element.95), calls=%async_computation | async-start | bytes 786432 | tf_op jit(solution)/shard_map/cond/branch_1_fun/all_to_all | solution.py:277
  61.3 26.1 %collective-permute-start.9 = (bf16[2,128,2048]{2,1,0:T(8,128)(2,1)S(1)}, bf16[2,128,2048]{2,1,0:T(8,128)(2,1)}, u32[]{:S(2)}, u32[]{:S(2)}) collective-permute-start(bf16[2,128,2048]{2,1,0:T(8,128)(2,1)S(1)} %get-tuple-element.101), channel_id=1, source_target_pairs={{0,1},{1,2},{2,3},{3,0},{4,5},{5,6},{6,7},{7,4},{8,9},{9,10},{10,1... | collective-permute-start | bytes 3145736 | tf_op jit(solution)/shard_map/cond/branch_1_fun/ppermute | solution.py:239
  62.2 9.9 %collective-permute-start.7 = (bf16[3750,128]{1,0:T(8,128)(2,1)}, bf16[3750,128]{1,0:T(8,128)(2,1)S(1)}, u32[]{:S(2)}, u32[]{:S(2)}) collective-permute-start(bf16[3750,128]{1,0:T(8,128)(2,1)} %get-tuple-element.97.refs_0_), channel_id=1, source_target_pairs={{0,16},{16,0},{32,48},{48,32},{64,80},{80,64},{96,112},{112,96},{1... | collective-permute-start | bytes 2880008 | tf_op jit(solution)/shard_map/cond/branch_1_fun/ppermute | solution.py:228
  63.6 8.5 %collective-permute-start.8 = (bf16[3750,128]{1,0:T(8,128)(2,1)}, bf16[3750,128]{1,0:T(8,128)(2,1)S(1)}, u32[]{:S(2)}, u32[]{:S(2)}) collective-permute-start(bf16[3750,128]{1,0:T(8,128)(2,1)} %get-tuple-element.98.refs_2_), channel_id=1, source_target_pairs={{0,16},{16,0},{32,48},{48,32},{64,80},{80,64},{96,112},{112,96},{1... | collective-permute-start | bytes 2880008 | tf_op jit(solution)/shard_map/cond/branch_1_fun/ppermute | solution.py:228
  63.6 23.9 %collective-permute-start.5 = (bf16[3750,128]{1,0:T(8,128)(2,1)}, bf16[3750,128]{1,0:T(8,128)(2,1)}, u32[]{:S(2)}, u32[]{:S(2)}) collective-permute-start(bf16[3750,128]{1,0:T(8,128)(2,1)} %get-tuple-element.97.refs_0_), channel_id=1, source_target_pairs={{0,32},{16,48},{32,64},{48,80},{64,96},{80,112},{96,128},{112,144}... | collective-permute-start | bytes 2880008 | tf_op jit(solution)/shard_map/cond/branch_1_fun/ppermute | solution.py:225
  63.6 23.9 %collective-permute-start.6 = (bf16[3750,128]{1,0:T(8,128)(2,1)}, bf16[3750,128]{1,0:T(8,128)(2,1)}, u32[]{:S(2)}, u32[]{:S(2)}) collective-permute-start(bf16[3750,128]{1,0:T(8,128)(2,1)} %get-tuple-element.98.refs_2_), channel_id=1, source_target_pairs={{0,224},{16,240},{32,0},{48,16},{64,32},{80,48},{96,64},{112,80},{... | collective-permute-start | bytes 2880008 | tf_op jit(solution)/shard_map/cond/branch_1_fun/ppermute | solution.py:225
  66.3 20.8 %all-to-all-start.1 = ((s16[16,48,512]{2,1,0:T(8,128)(2,1)}), s16[16,48,512]{2,1,0:T(8,128)(2,1)}, u32[]{:S(2)}, u32[]{:S(2)}) async-start(s16[16,48,512]{2,1,0:T(8,128)(2,1)} %get-tuple-element.100), calls=%async_computation.1 | async-start | bytes 1572864 | tf_op jit(solution)/shard_map/cond/branch_1_fun/all_to_all | solution.py:277
  87.5 17.0 %collective-permute-start.23 = (bf16[3750,128]{1,0:T(8,128)(2,1)}, bf16[3750,128]{1,0:T(8,128)(2,1)S(1)}, u32[]{:S(2)}, u32[]{:S(2)}) collective-permute-start(bf16[3750,128]{1,0:T(8,128)(2,1)} %get-tuple-element.104.refs_2_), channel_id=1, source_target_pairs={{0,16},{16,0},{32,48},{48,32},{64,80},{80,64},{96,112},{112,96},{1... | collective-permute-start | bytes 2880008 | tf_op jit(solution)/shard_map/cond/branch_1_fun/ppermute | solution.py:228
  89.3 15.7 %collective-permute-start.22 = (bf16[3750,128]{1,0:T(8,128)(2,1)}, bf16[3750,128]{1,0:T(8,128)(2,1)S(1)}, u32[]{:S(2)}, u32[]{:S(2)}) collective-permute-start(bf16[3750,128]{1,0:T(8,128)(2,1)} %get-tuple-element.103.refs_0_), channel_id=1, source_target_pairs={{0,16},{16,0},{32,48},{48,32},{64,80},{80,64},{96,112},{112,96},{1... | collective-permute-start | bytes 2880008 | tf_op jit(solution)/shard_map/cond/branch_1_fun/ppermute | solution.py:228
  90.8 23.0 %collective-permute-start.21 = (bf16[3750,128]{1,0:T(8,128)(2,1)S(1)}, bf16[3750,128]{1,0:T(8,128)(2,1)}, u32[]{:S(2)}, u32[]{:S(2)}) collective-permute-start(bf16[3750,128]{1,0:T(8,128)(2,1)S(1)} %broadcast_select_fusion), channel_id=1, source_target_pairs={{0,32},{16,240},{32,64},{48,16},{64,96},{80,48},{96,128},{112,80},... | collective-permute-start | bytes 2880008 | tf_op jit(solution)/shard_map/cond/branch_1_fun/ppermute | solution.py:242
  93.4 20.4 %all-to-all-start.3 = ((s16[16,48,512]{2,1,0:T(8,128)(2,1)}), s16[16,48,512]{2,1,0:T(8,128)(2,1)}, u32[]{:S(2)}, u32[]{:S(2)}) async-start(s16[16,48,512]{2,1,0:T(8,128)(2,1)} %get-tuple-element.106), calls=%async_computation.3 | async-start | bytes 1572864 | tf_op jit(solution)/shard_map/cond/branch_1_fun/all_to_all | solution.py:277
  101.3 11.8 %collective-permute-start.26 = (bf16[6,48,128]{2,1,0:T(8,128)(2,1)}, bf16[6,48,128]{2,1,0:T(8,128)(2,1)}, u32[]{:S(2)}, u32[]{:S(2)}) collective-permute-start(bf16[6,48,128]{2,1,0:T(8,128)(2,1)} %get-tuple-element.388), channel_id=1, source_target_pairs={{0,12},{1,13},{2,14},{3,15},{4,0},{5,1},{6,2},{7,3},{8,4},{9,5},{1... | collective-permute-start | bytes 221192 | tf_op jit(solution)/shard_map/cond/branch_1_fun/ppermute | solution.py:231
  103.9 9.3 %collective-permute-start.25 = (bf16[6,48,128]{2,1,0:T(8,128)(2,1)}, bf16[6,48,128]{2,1,0:T(8,128)(2,1)}, u32[]{:S(2)}, u32[]{:S(2)}) collective-permute-start(bf16[6,48,128]{2,1,0:T(8,128)(2,1)} %get-tuple-element.388), channel_id=1, source_target_pairs={{0,8},{1,9},{2,10},{3,11},{4,12},{5,13},{6,14},{7,15},{8,0},{9,1},... | collective-permute-start | bytes 221192 | tf_op jit(solution)/shard_map/cond/branch_1_fun/ppermute | solution.py:231
  104.4 9.4 %collective-permute-start.24 = (bf16[6,48,128]{2,1,0:T(8,128)(2,1)}, bf16[6,48,128]{2,1,0:T(8,128)(2,1)}, u32[]{:S(2)}, u32[]{:S(2)}) collective-permute-start(bf16[6,48,128]{2,1,0:T(8,128)(2,1)} %get-tuple-element.388), channel_id=1, source_target_pairs={{0,4},{1,5},{2,6},{3,7},{4,8},{5,9},{6,10},{7,11},{8,12},{9,13},{1... | collective-permute-start | bytes 221192 | tf_op jit(solution)/shard_map/cond/branch_1_fun/ppermute | solution.py:231
  113.8 2.8 %collective-permute-start.10 = (bf16[3750,128]{1,0:T(8,128)(2,1)}, bf16[3750,128]{1,0:T(8,128)(2,1)S(1)}, u32[]{:S(2)}, u32[]{:S(2)}) collective-permute-start(bf16[3750,128]{1,0:T(8,128)(2,1)} %get-tuple-element.113.refs_0_), channel_id=1, source_target_pairs={{0,16},{16,0},{32,48},{48,32},{64,80},{80,64},{96,112},{112,96},{1... | collective-permute-start | bytes 2880008 | tf_op jit(solution)/shard_map/cond/branch_1_fun/ppermute | solution.py:228
  123.3 24.3 %all-to-all-start.2 = ((s16[16,48,768]{2,1,0:T(8,128)(2,1)}), s16[16,48,768]{2,1,0:T(8,128)(2,1)}, u32[]{:S(2)}, u32[]{:S(2)}) async-start(s16[16,48,768]{2,1,0:T(8,128)(2,1)} %project.9), calls=%async_computation.2 | async-start | bytes 2359296 | tf_op jit(solution)/shard_map/cond/branch_1_fun/all_to_all | solution.py:277
  128.6 3.1 %collective-permute-start.13 = (bf16[2,128,2048]{2,1,0:T(8,128)(2,1)}, bf16[2,128,2048]{2,1,0:T(8,128)(2,1)}, u32[]{:S(2)}, u32[]{:S(2)}) collective-permute-start(bf16[2,128,2048]{2,1,0:T(8,128)(2,1)} %get-tuple-element.121), channel_id=1, source_target_pairs={{0,16},{16,0},{32,48},{48,32},{64,80},{80,64},{96,112},{112,96},{1... | collective-permute-start | bytes 3145736 | tf_op jit(solution)/shard_map/cond/branch_1_fun/ppermute | solution.py:228
  129.2 4.1 %collective-permute-start.12 = (bf16[2,128,2048]{2,1,0:T(8,128)(2,1)}, bf16[2,128,2048]{2,1,0:T(8,128)(2,1)}, u32[]{:S(2)}, u32[]{:S(2)}) collective-permute-start(bf16[2,128,2048]{2,1,0:T(8,128)(2,1)} %get-tuple-element.120), channel_id=1, source_target_pairs={{0,16},{16,0},{32,48},{48,32},{64,80},{80,64},{96,112},{112,96},{1... | collective-permute-start | bytes 3145736 | tf_op jit(solution)/shard_map/cond/branch_1_fun/ppermute | solution.py:228
  129.3 5.5 %collective-permute-start.11 = (bf16[2,128,2048]{2,1,0:T(8,128)(2,1)}, bf16[2,128,2048]{2,1,0:T(8,128)(2,1)}, u32[]{:S(2)}, u32[]{:S(2)}) collective-permute-start(bf16[2,128,2048]{2,1,0:T(8,128)(2,1)} %get-tuple-element.119), channel_id=1, source_target_pairs={{0,16},{16,0},{32,48},{48,32},{64,80},{80,64},{96,112},{112,96},{1... | collective-permute-start | bytes 3145736 | tf_op jit(solution)/shard_map/cond/branch_1_fun/ppermute | solution.py:228
  150.1 4.0 %collective-permute-start.16 = (bf16[10,48,128]{2,1,0:T(8,128)(2,1)}, bf16[10,48,128]{2,1,0:T(8,128)(2,1)}, u32[]{:S(2)}, u32[]{:S(2)}) collective-permute-start(bf16[10,48,128]{2,1,0:T(8,128)(2,1)} %get-tuple-element.410), channel_id=1, source_target_pairs={{0,12},{1,13},{2,14},{3,15},{4,0},{5,1},{6,2},{7,3},{8,4},{9,5},{1... | collective-permute-start | bytes 368648 | tf_op jit(solution)/shard_map/cond/branch_1_fun/ppermute | solution.py:231
  150.4 5.6 %collective-permute-start.15 = (bf16[10,48,128]{2,1,0:T(8,128)(2,1)}, bf16[10,48,128]{2,1,0:T(8,128)(2,1)}, u32[]{:S(2)}, u32[]{:S(2)}) collective-permute-start(bf16[10,48,128]{2,1,0:T(8,128)(2,1)} %get-tuple-element.410), channel_id=1, source_target_pairs={{0,8},{1,9},{2,10},{3,11},{4,12},{5,13},{6,14},{7,15},{8,0},{9,1},... | collective-permute-start | bytes 368648 | tf_op jit(solution)/shard_map/cond/branch_1_fun/ppermute | solution.py:231
  151.4 6.1 %collective-permute-start.14 = (bf16[10,48,128]{2,1,0:T(8,128)(2,1)}, bf16[10,48,128]{2,1,0:T(8,128)(2,1)}, u32[]{:S(2)}, u32[]{:S(2)}) collective-permute-start(bf16[10,48,128]{2,1,0:T(8,128)(2,1)} %get-tuple-element.410), channel_id=1, source_target_pairs={{0,4},{1,5},{2,6},{3,7},{4,8},{5,9},{6,10},{7,11},{8,12},{9,13},{1... | collective-permute-start | bytes 368648 | tf_op jit(solution)/shard_map/cond/branch_1_fun/ppermute | solution.py:231
  181.0 13.0 %all-to-all-start.5 = ((f32[16,1,16]{2,1,0:T(1,128)}), f32[16,1,16]{2,1,0:T(1,128)S(1)}, u32[]{:S(2)}, u32[]{:S(2)}) async-start(f32[16,1,16]{2,1,0:T(1,128)} %broadcast_in_dim.30), calls=%async_computation.5 | async-start | bytes 16384 | tf_op jit(solution)/shard_map/all_to_all | solution.py:331
  (3 other events, 39.8 us)
